TPU v7x, 256 devices: a whole 4x4x8 slice. The times are simulated.
256 devices in a mesh: wide: 16 (over x, z_lo), narrow: 16 (over z_hi, y, core).
Axes of the slice: x: 4, y: 4, z: 8 (z_hi: 2, z_lo: 4; z = z_hi * 4 + z_lo), core: 2. Of those that a mesh axis runs over, the one named last changes fastest.
Arguments:
- basis: float32 [65536, 8192], P('wide', 'narrow'), may hold values from -0.0234375 to 0.0234375
- conf_values: float32 [8192], P('narrow'), may hold values from 0.5 to 8
- task_basis: float32 [128, 128], replicated, may hold values from -0.5 to 0.5
- task_values: float32 [128], replicated, may hold values from 0.5 to 4
- noise: float32 [1], replicated, may hold values from 0.2 to 1
- observations: float32 [65536, 128], P(('wide', 'narrow')), may hold values from -6 to 6
- train_codes: int32 [65536], P(('wide', 'narrow')), may hold values from 0 to 1048575
- length_scales: float32 [10], replicated, may hold values from 0.03 to 0.3
- signal: float32 [1], replicated, may hold values from 0.03 to 0.1
- cand_codes: int32 [32768], P('wide'), may hold values from 0 to 1048575
Outputs:
- coefficients: float32 [65536, 128], P(('wide', 'narrow'))
- means: float32 [32768, 128], P(('wide', 'narrow'))
All inputs are finite; a program needn't handle non-finite values.
Results may differ from a plain program's by a relative error of at most 0.0003.
Values sent between devices are 32-bit elements; how exact they have to be, the bound alone decides.
No kernel may reach another device: no remote copies, remote signals or barrier semaphores. Data moves between devices by JAX's collectives and lax.ppermute only.
A program may use at most 128 MiB of HBM per device.

v0:
```python
import functools
import math

import jax
import jax.numpy as jnp
from jax import lax
from jax.experimental import pallas as pl
from jax.experimental.pallas import tpu as pltpu
from jax.sharding import PartitionSpec as P

F32 = jnp.float32
BF16 = jnp.bfloat16
VM = pltpu.VMEM
MIB = 1 << 20


def far_memory(value):
    return pltpu.with_memory_space_constraint(value, pltpu.HBM)


def split(x):
    high = x.astype(BF16)
    return high, (x - high.astype(F32)).astype(BF16)


def mul(a, b, dims=(((1,), (0,)), ((), ()))):
    return lax.dot_general(a, b, dims, preferred_element_type=F32)


def mul3(a, b, dims=(((1,), (0,)), ((), ()))):
    ah, al = split(a)
    bh, bl = split(b)
    return mul(ah, bh, dims) + (mul(ah, bl, dims) + mul(al, bh, dims))


NT = (((1,), (1,)), ((), ()))


def swap(value, axis, bits):
    return lax.ppermute(value, axis, [(i, i ^ bits) for i in range(16)])


def full(shape):
    return pl.BlockSpec(shape, lambda *_: (0,) * len(shape))


def params(mib):
    return pltpu.CompilerParams(vmem_limit_bytes=mib * MIB)


def here(count):
    return [pl.BlockSpec(memory_space=VM)] * count


def scalars(count):
    return [pl.BlockSpec(memory_space=pltpu.SMEM)] * count


def anywhere(count):
    return [pl.BlockSpec(memory_space=pl.ANY)] * count


def struct(shape, dtype=F32):
    return jax.ShapeDtypeStruct(shape, dtype)


def cost(flops=0, moved=0, transcendentals=0):
    return pl.CostEstimate(flops=flops, bytes_accessed=moved, transcendentals=transcendentals)


def halves_kernel(basis, high, low, held, arrived):
    def fetch(step):
        rows = pl.ds(pl.multiple_of(step * 512, 512), 512)
        return pltpu.make_async_copy(basis.at[rows, :], held.at[rows, :], arrived.at[step])

    for step in range(8):
        fetch(step).start()

    def part(step, carry):
        fetch(step).wait()
        rows = pl.ds(pl.multiple_of(step * 512, 512), 512)
        h, l = split(held[rows, :])
        high[rows, :] = h
        low[rows, :] = l
        return carry

    lax.fori_loop(0, 8, part, 0)


def halves(basis):
    return pl.pallas_call(
        halves_kernel,
        in_specs=anywhere(1),
        out_specs=here(2),
        out_shape=[struct((4096, 512), BF16)] * 2,
        scratch_shapes=[pltpu.VMEM((4096, 512), F32), pltpu.SemaphoreType.DMA((8,))],
        compiler_params=params(20),
        cost_estimate=cost(1, 1),
        name="basis_halves",
    )(far_memory(basis))


def stack_kernel(count, *refs):
    for place in range(count):
        refs[-1][place] = refs[place][...]


def stack(values, after):
    return pl.pallas_call(
        functools.partial(stack_kernel, len(values)),
        in_specs=here(len(values)) + anywhere(len(after)),
        out_specs=here(1)[0],
        out_shape=struct((len(values), *values[0].shape)),
        compiler_params=params(3),
        name="stack",
    )(*values, *after)


def own_kernel(where, observations, codes, out):
    out[0:128, :] = observations[...].T
    out[128:136, :] = jnp.broadcast_to(codes[...].astype(F32), (8, 256))


def own_block(where, observations, codes):
    return pl.pallas_call(
        own_kernel,
        grid=(1,),
        in_specs=scalars(1) + [full((256, 128)), full((1, 256))],
        out_specs=full((136, 256)),
        out_shape=struct((136, 256)),
        compiler_params=params(2),
        name="own_observations",
    )(where, far_memory(observations), far_memory(codes[None]))


def project_part(me, high, low, total, near, other, first, far):
    def step(i, total):
        for part in range(2):
            for core, ref in enumerate((near, other)):
                slot = (first + i * 2 + part) * 2 + core + far * 8
                rows = pl.ds(pl.multiple_of((me ^ slot) * 256, 256), 256)
                oh, ol = split(ref[i * 2 + part, 0:128, :])
                both = mul(jnp.concatenate([oh, ol], axis=0), high[rows, :])
                total = total + both[:128] + (both[128:] + mul(oh, low[rows, :]))
        return total

    return lax.fori_loop(0, near.shape[0] // 2, step, total)


def near_kernel(where, high, low, near, other, out):
    out[...] = project_part(where[0], high, low, jnp.zeros((128, 512), F32), near, other, 0, 0)


def project_near(where, high, low, near, other):
    return pl.pallas_call(
        near_kernel,
        in_specs=scalars(1) + here(4),
        out_specs=here(1)[0],
        out_shape=struct((128, 512)),
        compiler_params=params(16),
        cost_estimate=cost(1, 1),
        name="project_near",
    )(where, high, low, near, other)


def project_kernel(where, high, low, task_basis, cand, before, near0, other0, near1, other1, *refs):
    outs, rotated = refs[:4], refs[4]
    me, x = where[0], where[1] // 4
    total = project_part(me, high, low, before[...], near0, other0, 0, 1)
    total = project_part(me, high, low, total, near1, other1, 2, 1)
    rotated[...] = mul3(task_basis[...].T, total)
    columns = pl.ds(pl.multiple_of(me * 128, 128), 128)
    codes = jnp.broadcast_to(cand[:, columns].astype(F32), (8, 128))
    for d in range(4):
        outs[d][0:32, :] = rotated[pl.ds(pl.multiple_of((x ^ d) * 32, 32), 32), :]
        outs[d][32:40, :] = jnp.concatenate([codes] * 4, axis=1)


def project(where, high, low, task_basis, cand, before, pairs):
    return pl.pallas_call(
        project_kernel,
        in_specs=scalars(1) + here(9),
        out_specs=here(4),
        out_shape=[struct((40, 512))] * 4,
        scratch_shapes=[pltpu.VMEM((128, 512), F32)],
        compiler_params=params(16),
        cost_estimate=cost(1, 1),
        name="project",
    )(where, high, low, task_basis, cand, before, *pairs)


def collect_kernel(own, a, b, c, out):
    out[0:32, :] = (own[0:32, :] + a[0:32, :]) + (b[0:32, :] + c[0:32, :])
    rows = [ref[32:33, :] for ref in (own, a, b, c)]
    out[32:40, :] = jnp.concatenate(rows + rows, axis=0)


def collect(pieces):
    return pl.pallas_call(
        collect_kernel,
        in_specs=here(4),
        out_specs=here(1)[0],
        out_shape=struct((40, 512)),
        compiler_params=params(2),
        name="sum_over_x",
    )(*pieces)


def scale_kernel(where, noise, conf_values, task_values, own, a, b, c, out, codes, column):
    column[...] = jnp.broadcast_to(task_values[...], (128, 128)).T
    rows = pl.ds(pl.multiple_of(where[1] // 4 * 32, 32), 32)
    total = (own[0:32, :] + a[0:32, :]) + (b[0:32, :] + c[0:32, :])
    out[...] = total / (conf_values[...] * column[rows, 0:1] + noise[0])
    for far in range(4):
        for near, ref in enumerate((own, a, b, c)):
            slot = far * 4 + near
            codes[slot : slot + 1, :] = ref[32 + far : 33 + far, 0:128]


def scale(where, noise, conf_values, task_values, pieces):
    return pl.pallas_call(
        scale_kernel,
        in_specs=scalars(2) + here(6),
        out_specs=here(2),
        out_shape=[struct((32, 512)), struct((16, 128))],
        scratch_shapes=[pltpu.VMEM((128, 128), F32)],
        compiler_params=params(2),
        name="scale",
    )(where, noise, conf_values, task_values, *pieces)


def back_kernel(where, task_basis, a, b, c, d, *refs):
    out, scaled = refs[-2:]
    x = where[1] // 4
    for far, ref in enumerate((a, b, c, d)):
        scaled[pl.ds(pl.multiple_of((x ^ far) * 32, 32), 32), :] = ref[...]
    kh, kl = split(mul3(scaled[...].T, task_basis[...], NT))
    out[:, 0:128] = kh
    out[:, 128:256] = kl


def rotate_back(where, task_basis, pieces, after):
    return pl.pallas_call(
        back_kernel,
        in_specs=scalars(1) + here(5) + anywhere(len(after)),
        out_specs=here(1)[0],
        out_shape=struct((512, 256), BF16),
        scratch_shapes=[pltpu.VMEM((128, 512), F32)],
        compiler_params=params(4),
        name="rotate_back",
    )(where, task_basis, *pieces, *after)


def expand_kernel(core, far, where, high, low, wide, *refs):
    def step(i, carry):
        for d in (i * 2, i * 2 + 1):
            slot = d * 2 + core + far * 8
            rows = pl.ds(pl.multiple_of((where[0] ^ slot) * 256, 256), 256)
            both = mul(high[rows, :], wide[...])
            refs[-1][d] = both[:, :128] + (both[:, 128:] + mul(low[rows, :], wide[:, 0:128]))
        return carry

    lax.fori_loop(0, 2, step, 0)


def expand(core, far, where, high, low, wide, after):
    return pl.pallas_call(
        functools.partial(expand_kernel, core, far),
        in_specs=scalars(1) + here(3) + anywhere(len(after)),
        out_specs=here(1)[0],
        out_shape=struct((4, 256, 128)),
        compiler_params=params(14),
        cost_estimate=cost(1, 1),
        name="expand",
    )(where, high, low, wide, *after)


def pairs_kernel(mine, theirs, *outs):
    for d in range(4):
        outs[d][...] = mine[d] + theirs[d]


def sum_pairs(mine, theirs):
    return pl.pallas_call(
        pairs_kernel,
        in_specs=here(2),
        out_specs=here(4),
        out_shape=[struct((256, 128))] * 4,
        compiler_params=params(6),
        name="sum_over_core",
    )(mine, theirs)


def sum_kernel(count, copies, *refs):
    total = refs[0][...]
    for ref in refs[1:count]:
        total = total + ref[...]
    for ref in refs[-copies:]:
        ref[...] = total


def sum_blocks(blocks, after, copies=1):
    return pl.pallas_call(
        functools.partial(sum_kernel, len(blocks), copies),
        in_specs=here(len(blocks)) + anywhere(len(after)),
        out_specs=here(copies),
        out_shape=[struct((256, 128))] * copies,
        compiler_params=params(2),
        name="sum_over_y",
    )(*blocks, *after)


def row_digit(codes, k):
    part = (k >= 40).astype(jnp.int32) + (k >= 80).astype(jnp.int32) + (k >= 120).astype(jnp.int32)
    rest = k - 40 * part
    return part, rest & 3, lax.shift_right_logical(codes, 2 * lax.shift_right_logical(rest, 2)) & 3


def onehot_kernel(length_scales, codes, out, lengths):
    k = lax.broadcasted_iota(jnp.int32, (128, 128), 0)
    part, _, _ = row_digit(k, k)
    feature = lax.shift_right_logical(k - 40 * part, 2)
    value = jnp.zeros((128, 128), F32)
    for place in range(10):
        value = jnp.where(feature == place, length_scales[place] * (-1.0 / math.log(2.0)), value)
    lengths[...] = value

    for slot in range(16):
        row = codes[slot : slot + 1, :].astype(jnp.int32)
        _, level, digit = row_digit(jnp.broadcast_to(row, (128, 128)), k)
        hot = jnp.where(digit == level, 1.0, 0.0).astype(F32)
        out[slot * 128 : slot * 128 + 128, :] = hot.T.astype(BF16)


def onehot(length_scales, codes):
    return pl.pallas_call(
        onehot_kernel,
        in_specs=scalars(1) + here(1),
        out_specs=here(2),
        out_shape=[struct((2048, 128), BF16), struct((128, 128))],
        compiler_params=params(2),
        name="candidate_levels",
    )(length_scales, codes)


def cross_kernel(firsts, hot, lengths, *refs):
    count = len(firsts)
    outs, table = refs[-1 - 2 * count : -1], refs[-1]
    k = lax.broadcasted_iota(jnp.int32, (128, 256), 0)
    length = jnp.concatenate([lengths[...], lengths[...]], axis=1)
    for place, first in enumerate(firsts):
        for part in range(2):
            row = refs[place][first + part, 128:129, :].astype(jnp.int32)
            piece, level, digit = row_digit(jnp.broadcast_to(row, (128, 256)), k)
            differ = (level - digit).astype(F32)
            value = length * differ * differ
            one = value.astype(BF16).astype(F32)
            two = (value - one).astype(BF16).astype(F32)
            three = value - one - two
            value = jnp.where(piece == 0, one, jnp.where(piece == 1, two, jnp.where(piece == 2, three, 0.0)))
            table[:, part * 256 : part * 256 + 256] = value.astype(BF16)

        def step(i, carry, high=outs[2 * place], low=outs[2 * place + 1]):
            for part in range(2):
                rows = pl.ds(pl.multiple_of(i * (256 * 2) + part * 256, 256), 256)
                h, l = split(jnp.exp2(mul(hot[rows, :], table[...])))
                high[rows, :] = h
                low[rows, :] = l
            return carry

        lax.fori_loop(0, 8 // 2, step, 0)


def cross_halves(hot, lengths, sources, after):
    arrays, firsts = zip(*sources)
    count = len(sources)
    outs = pl.pallas_call(
        functools.partial(cross_kernel, firsts),
        in_specs=here(2 + count) + anywhere(len(after)),
        out_specs=here(2 * count),
        out_shape=[struct((2048, 512), BF16)] * (2 * count),
        scratch_shapes=[pltpu.VMEM((128, 512), BF16)],
        compiler_params=params(16),
        cost_estimate=cost(1, 1),
        name="cross",
    )(hot, lengths, *arrays, *after)
    return [tuple(outs[2 * place : 2 * place + 2]) for place in range(count)]


def predict_kernel(first, near_first, has_total, near, other, h0, l0, h1, l1, *refs):
    total, out, wide = (refs[0] if has_total else None), refs[-2], refs[-1]
    for core, ref in enumerate((near, other)):
        for part in range(2):
            rows = pl.ds(core * 512 + part * 256, 256)
            wh, wl = split(ref[near_first + part])
            wide[rows, 0:128] = wh
            wide[rows, 128:256] = wl

    def step(i, carry):
        for part in range(2):
            start = i * 512 + part * 256
            rows = pl.ds(pl.multiple_of(first + start, 256), 256)
            both = mul(h0[rows, :], wide[0:512, :]) + mul(h1[rows, :], wide[512:1024, :])
            rest = mul(l0[rows, :], wide[0:512, 0:128]) + mul(l1[rows, :], wide[512:1024, 0:128])
            value = both[:, :128] + (both[:, 128:] + rest)
            out[pl.ds(pl.multiple_of(start, 256), 256), :] = value if total is None else total[rows, :] + value
        return carry

    lax.fori_loop(0, out.shape[0] // 512, step, 0)


def predict(near, other, near_first, cross0, cross1, total, first, count, after=()):
    extra = [] if total is None else [total]
    return pl.pallas_call(
        functools.partial(predict_kernel, first, near_first, total is not None),
        in_specs=here(6 + len(extra)) + anywhere(len(after)),
        out_specs=here(1)[0],
        out_shape=struct((count, 128)),
        scratch_shapes=[pltpu.VMEM((1024, 256), BF16)],
        compiler_params=params(14),
        cost_estimate=cost(1, 1),
        name="predict",
    )(near, other, *cross0, *cross1, *extra, *after)


def quarter_kernel(a, b, c, d, *outs):
    for g in range(4):
        rows = pl.ds(g * 128, 128)
        outs[g][...] = (a[rows, :] + b[rows, :]) + (c[rows, :] + d[rows, :])


def sum_quarters(blocks):
    return pl.pallas_call(
        quarter_kernel,
        in_specs=here(4),
        out_specs=here(4),
        out_shape=[struct((128, 128))] * 4,
        compiler_params=params(3),
        name="means_over_x",
    )(*blocks)


def finish_kernel(signal, a, b, c, d, task_basis, task_values, out):
    kernel = mul3(task_basis[...] * task_values[...], task_basis[...], NT)
    out[...] = signal[0] * mul3((a[...] + b[...]) + (c[...] + d[...]), kernel)


def finish(signal, parts, task_basis, task_values):
    return pl.pallas_call(
        finish_kernel,
        in_specs=scalars(1) + here(6),
        out_specs=here(1)[0],
        out_shape=struct((128, 128)),
        compiler_params=params(2),
        name="finish",
    )(signal, *parts, task_basis, task_values)


def local(
    basis,
    conf_values,
    task_basis,
    task_values,
    noise,
    observations,
    train_codes,
    length_scales,
    signal,
    cand_codes,
):
    n = lax.axis_index("narrow").astype(jnp.int32)
    w = lax.axis_index("wide").astype(jnp.int32)
    where = jnp.stack([n, w])

    own = own_block(where, observations, train_codes)
    high, low = halves(basis)
    near = stack([own] + [swap(own, "narrow", 2 * d) for d in (1, 2, 3)], [high])
    other = swap(near, "narrow", 1)
    before = project_near(where, high, low, near, other)
    mirror = swap(own, "narrow", 8)
    far = [mirror] + [swap(mirror, "narrow", 2 * d) for d in (1, 2, 3)]
    pairs = []
    for pair in (stack(far[:2], []), stack(far[2:], [])):
        pairs += [pair, swap(pair, "narrow", 1)]
    pieces = project(where, high, low, task_basis, cand_codes[None], before, pairs)
    mine = collect([pieces[0]] + [swap(pieces[d], "wide", 4 * d) for d in (1, 2, 3)])
    arrived = [mine] + [swap(mine, "wide", d) for d in (1, 2, 3)]
    scaled, codes = scale(where, noise, conf_values[None], task_values[None], arrived)
    quarters = [scaled] + [swap(scaled, "wide", 4 * d) for d in (1, 2, 3)]

    hot, lengths = onehot(length_scales, codes)
    sources = [(near, 0), (other, 0), (near, 2), (other, 2)] + [(array, 0) for array in pairs]
    crosses = cross_halves(hot, lengths, sources[:3], [])
    wide = rotate_back(where, task_basis, quarters, [crosses[0][0]])
    odd = expand(1, 1, where, high, low, wide, [])
    even = expand(0, 1, where, high, low, wide, [])
    sums = sum_pairs(even, swap(odd, "narrow", 1))
    odd = expand(1, 0, where, high, low, wide, [sums[0]])
    even = expand(0, 0, where, high, low, wide, [sums[0]])
    later = sum_pairs(even, swap(odd, "narrow", 1))
    total = [sums[0]] + [swap(sums[d], "narrow", 2 * d) for d in (1, 2, 3)]
    total = sum_blocks(total, [later[0]])[0]
    mirror = swap(total, "narrow", 8)
    crosses += cross_halves(hot, lengths, sources[3:6], [total])
    total = [later[0]] + [swap(later[d], "narrow", 2 * d) for d in (1, 2, 3)]
    block, coefficients = sum_blocks(total + [mirror], [crosses[5][0]], 2)

    mirror = swap(block, "narrow", 8)
    crosses += cross_halves(hot, lengths, sources[6:], [block])
    near = stack([block] + [swap(block, "narrow", 2 * d) for d in (1, 2, 3)], [mirror, crosses[6][0]])
    other = swap(near, "narrow", 1)
    start = predict(near, other, 0, *crosses[0:2], None, 0, 2048)
    means = predict(near, other, 2, *crosses[2:4], start, 0, 2048)
    far = [mirror] + [swap(mirror, "narrow", 2 * d) for d in (1, 2, 3)]
    near = stack(far[:2], [start])
    other = swap(near, "narrow", 1)
    after = [means]
    means = predict(near, other, 0, *crosses[4:6], means, 0, 2048)
    near = stack(far[2:], after)
    other = swap(near, "narrow", 1)
    last, after = {}, []
    for g in (2, 1, 3, 0):
        last[g] = predict(near, other, 0, *crosses[6:8], means, g * 512, 512, after)
        after = [last[g]]
    quarters = sum_quarters([last[0]] + [swap(last[g], "wide", 4 * g) for g in (2, 1, 3)])
    ends = [quarters[0]] + [swap(quarters[g], "wide", g) for g in (1, 2, 3)]
    return coefficients, finish(signal, ends, task_basis, task_values[None])


def solution(mesh):
    return jax.shard_map(
        local,
        mesh=mesh,
        in_specs=(
            P("wide", "narrow"),
            P("narrow"),
            P(),
            P(),
            P(),
            P(("wide", "narrow"), None),
            P(("wide", "narrow")),
            P(),
            P(),
            P("wide"),
        ),
        out_specs=(P(("wide", "narrow"), None), P(("wide", "narrow"), None)),
        check_vma=False,
    )
```

profile of v0, /device:TPU:32, one launch (start us, length us, event | category | flops | bytes accessed | tf_op | source)
XLA Modules:
  0.0 154.5 jit_solution(4527584771290433864)
XLA Ops:
  1.7 1.7 %collective-permute-start = (f32[136,256]{1,0:T(8,128)S(1)}, f32[136,256]{1,0:T(8,128)S(1)}, u32[]{:S(2)}, u32[]{:S(2)}) collective-permute-start(f32[136,256]{1,0:T(8,128)S(1)} %own_observations.1.refs_0_), channel_id=1, source_target_pairs={{0,2},{1,3},{2,0},{3,1},{4,6},{5,7},{6,4},{7,5},{8,10},{9,11},{10,... | collective-permute-start | bytes 417800 | tf_op jit(solution)/shard_map/ppermute | solution.py:40
  3.4 2.9 %collective-permute-start.1 = (f32[136,256]{1,0:T(8,128)S(1)}, f32[136,256]{1,0:T(8,128)S(1)}, u32[]{:S(2)}, u32[]{:S(2)}) collective-permute-start(f32[136,256]{1,0:T(8,128)S(1)} %own_observations.1.refs_0_), channel_id=1, source_target_pairs={{0,4},{1,5},{2,6},{3,7},{4,0},{5,1},{6,2},{7,3},{8,12},{9,13},{10,... | collective-permute-start | bytes 417800 | tf_op jit(solution)/shard_map/ppermute | solution.py:40
  6.5 6.3 %collective-permute-start.4 = (f32[136,256]{1,0:T(8,128)S(1)}, f32[136,256]{1,0:T(8,128)S(1)}, u32[]{:S(2)}, u32[]{:S(2)}) collective-permute-start(f32[136,256]{1,0:T(8,128)S(1)} %own_observations.1.refs_0_), channel_id=1, source_target_pairs={{0,8},{1,9},{2,10},{3,11},{4,12},{5,13},{6,14},{7,15},{8,0},{9,1},... | collective-permute-start | bytes 417800 | tf_op jit(solution)/shard_map/ppermute | solution.py:40
  12.8 3.6 %basis_halves.1 = (bf16[4096,512]{1,0:T(8,128)(2,1)S(1)}, bf16[4096,512]{1,0:T(8,128)(2,1)S(1)}) custom-call(f32[4096,512]{1,0:T(8,128)} %basis.1), custom_call_target="tpu_custom_call" | custom-call | flops 1 | bytes 1 | tf_op jit(solution)/shard_map/basis_halves/pallas_call | solution.py:91
  16.6 1.9 %collective-permute-done.4.refs_0_ = f32[136,256]{1,0:T(8,128)S(1)} collective-permute-done((f32[136,256]{1,0:T(8,128)S(1)}, f32[136,256]{1,0:T(8,128)S(1)}, u32[]{:S(2)}, u32[]{:S(2)}) %collective-permute-start.4) | collective-permute-done | bytes 139296 | tf_op jit(solution)/shard_map/ppermute | solution.py:40
  18.5 1.9 %collective-permute-start.7 = (f32[136,256]{1,0:T(8,128)S(1)}, f32[136,256]{1,0:T(8,128)S(1)}, u32[]{:S(2)}, u32[]{:S(2)}) collective-permute-start(f32[136,256]{1,0:T(8,128)S(1)} %collective-permute-done.4.refs_0_), channel_id=1, source_target_pairs={{0,4},{1,5},{2,6},{3,7},{4,0},{5,1},{6,2},{7,3},{8,12},{9,13},{10,... | collective-permute-start | bytes 417800 | tf_op jit(solution)/shard_map/ppermute | solution.py:40
  20.5 1.1 collective-permute-start.8
  22.4 4.0 %collective-permute-done.7.refs_0_ = f32[136,256]{1,0:T(8,128)S(1)} collective-permute-done((f32[136,256]{1,0:T(8,128)S(1)}, f32[136,256]{1,0:T(8,128)S(1)}, u32[]{:S(2)}, u32[]{:S(2)}) %collective-permute-start.7) | collective-permute-done | bytes 139296 | tf_op jit(solution)/shard_map/ppermute | solution.py:40
  28.1 1.7 %project_near.1.before = f32[128,512]{1,0:T(8,128)S(1)} custom-call(s32[2]{0:T(128)S(1)} %pad_add_fusion.where, bf16[4096,512]{1,0:T(8,128)(2,1)S(1)} %get-tuple-element.42.refs_4_.high, bf16[4096,512]{1,0:T(8,128)(2,1)S(1)} %get-tuple-element.43.low, f32[4,136,256]{2,1,0:T(8,128)S(1)} %stack.18.near.refs_0_.refs_2_, ...), custom_call_target="tpu_custom_call" | custom-call | flops 1 | bytes 1 | tf_op jit(solution)/shard_map/project_near/pallas_call | solution.py:155
  29.9 1.8 %project.1 = (f32[40,512]{1,0:T(8,128)S(1)}, f32[40,512]{1,0:T(8,128)S(1)}, f32[40,512]{1,0:T(8,128)S(1)}, f32[40,512]{1,0:T(8,128)S(1)}) custom-call(s32[2]{0:T(128)S(1)} %pad_add_fusion.where, bf16[4096,512]{1,0:T(8,128)(2,1)S(1)} %get-tuple-element.42.refs_4_.high, bf16[4096,512]{1,0:T(8,128)(2,1)S(1)} %get-tuple-element.43.low, f32[128,128]{1,0:T(8,128)S(1)} %copy-done, ...), custom_call_target="tpu_custom_call" | custom-call | flops 1 | bytes 1 | tf_op jit(solution)/shard_map/project/pallas_call | solution.py:180
  31.7 1.6 %collective-permute-start.10 = (f32[40,512]{1,0:T(8,128)S(1)}, f32[40,512]{1,0:T(8,128)S(1)}, u32[]{:S(2)}, u32[]{:S(2)}) collective-permute-start(f32[40,512]{1,0:T(8,128)S(1)} %get-tuple-element.45), channel_id=1, source_target_pairs={{0,64},{16,80},{32,96},{48,112},{64,0},{80,16},{96,32},{112,48},{1... | collective-permute-start | bytes 245768 | tf_op jit(solution)/shard_map/ppermute | solution.py:40
  33.2 2.7 %collective-permute-start.11 = (f32[40,512]{1,0:T(8,128)S(1)}, f32[40,512]{1,0:T(8,128)S(1)}, u32[]{:S(2)}, u32[]{:S(2)}) collective-permute-start(f32[40,512]{1,0:T(8,128)S(1)} %get-tuple-element.46), channel_id=1, source_target_pairs={{0,128},{16,144},{32,160},{48,176},{64,192},{80,208},{96,224},{112... | collective-permute-start | bytes 245768 | tf_op jit(solution)/shard_map/ppermute | solution.py:40
  36.4 3.8 %collective-permute-done.11.b = f32[40,512]{1,0:T(8,128)S(1)} collective-permute-done((f32[40,512]{1,0:T(8,128)S(1)}, f32[40,512]{1,0:T(8,128)S(1)}, u32[]{:S(2)}, u32[]{:S(2)}) %collective-permute-start.11) | collective-permute-done | bytes 81952 | tf_op jit(solution)/shard_map/ppermute | solution.py:40
  40.3 1.7 %collective-permute-done.12.c = f32[40,512]{1,0:T(8,128)S(1)} collective-permute-done((f32[40,512]{1,0:T(8,128)S(1)}, f32[40,512]{1,0:T(8,128)S(1)}, u32[]{:S(2)}, u32[]{:S(2)}) %collective-permute-start.12) | collective-permute-done | bytes 81952 | tf_op jit(solution)/shard_map/ppermute | solution.py:40
  42.0 1.1 collective-permute-start.13
  43.1 2.6 %collective-permute-start.14 = (f32[40,512]{1,0:T(8,128)S(1)}, f32[40,512]{1,0:T(8,128)S(1)}, u32[]{:S(2)}, u32[]{:S(2)}) collective-permute-start(f32[40,512]{1,0:T(8,128)S(1)} %sum_over_x.1.own), channel_id=1, source_target_pairs={{0,32},{16,48},{32,0},{48,16},{64,96},{80,112},{96,64},{112,80},{1... | collective-permute-start | bytes 245768 | tf_op jit(solution)/shard_map/ppermute | solution.py:40
  47.1 3.8 %collective-permute-done.14.b = f32[40,512]{1,0:T(8,128)S(1)} collective-permute-done((f32[40,512]{1,0:T(8,128)S(1)}, f32[40,512]{1,0:T(8,128)S(1)}, u32[]{:S(2)}, u32[]{:S(2)}) %collective-permute-start.14) | collective-permute-done | bytes 81952 | tf_op jit(solution)/shard_map/ppermute | solution.py:40
  50.9 1.9 %collective-permute-done.15.c = f32[40,512]{1,0:T(8,128)S(1)} collective-permute-done((f32[40,512]{1,0:T(8,128)S(1)}, f32[40,512]{1,0:T(8,128)S(1)}, u32[]{:S(2)}, u32[]{:S(2)}) %collective-permute-start.15) | collective-permute-done | bytes 81952 | tf_op jit(solution)/shard_map/ppermute | solution.py:40
  53.6 2.6 %collective-permute-start.17 = (f32[32,512]{1,0:T(8,128)S(1)}, f32[32,512]{1,0:T(8,128)S(1)}, u32[]{:S(2)}, u32[]{:S(2)}) collective-permute-start(f32[32,512]{1,0:T(8,128)S(1)} %get-tuple-element.48.a), channel_id=1, source_target_pairs={{0,128},{16,144},{32,160},{48,176},{64,192},{80,208},{96,224},{112... | collective-permute-start | bytes 196616 | tf_op jit(solution)/shard_map/ppermute | solution.py:40
  56.3 2.1 %collective-permute-start.18 = (f32[32,512]{1,0:T(8,128)S(1)}, f32[32,512]{1,0:T(8,128)S(1)}, u32[]{:S(2)}, u32[]{:S(2)}) collective-permute-start(f32[32,512]{1,0:T(8,128)S(1)} %get-tuple-element.48.a), channel_id=1, source_target_pairs={{0,192},{16,208},{32,224},{48,240},{64,128},{80,144},{96,160},{112... | collective-permute-start | bytes 196616 | tf_op jit(solution)/shard_map/ppermute | solution.py:40
  59.1 4.4 %cross.3 = (bf16[2048,512]{1,0:T(8,128)(2,1)S(1)}, bf16[2048,512]{1,0:T(8,128)(2,1)S(1)}, bf16[2048,512]{1,0:T(8,128)(2,1)S(1)}, bf16[2048,512]{1,0:T(8,128)(2,1...) custom-call(bf16[2048,128]{1,0:T(8,128)(2,1)S(1)} %get-tuple-element.50.hot, ...), custom_call_target="tpu_custom_call" | custom-call | flops 1 | bytes 1 | tf_op jit(solution)/shard_map/cross/pallas_call | solution.py:377
  64.5 1.4 expand.5
  66.0 1.4 expand.4.mine
  67.9 1.4 expand.7
  69.7 3.6 %collective-permute-start.25 = (f32[256,128]{1,0:T(8,128)S(1)}, f32[256,128]{1,0:T(8,128)S(1)}, u32[]{:S(2)}, u32[]{:S(2)}) collective-permute-start(f32[256,128]{1,0:T(8,128)S(1)} %get-tuple-element.59), channel_id=1, source_target_pairs={{0,4},{1,5},{2,6},{3,7},{4,0},{5,1},{6,2},{7,3},{8,12},{9,13},{10,... | collective-permute-start | bytes 393224 | tf_op jit(solution)/shard_map/ppermute | solution.py:40
  74.3 1.4 expand.6.mine
  75.9 4.1 %collective-permute-done.25.refs_2_ = f32[256,128]{1,0:T(8,128)S(1)} collective-permute-done((f32[256,128]{1,0:T(8,128)S(1)}, f32[256,128]{1,0:T(8,128)S(1)}, u32[]{:S(2)}, u32[]{:S(2)}) %collective-permute-start.25) | collective-permute-done | bytes 131104 | tf_op jit(solution)/shard_map/ppermute | solution.py:40
  80.0 2.4 %collective-permute-done.26.refs_3_ = f32[256,128]{1,0:T(8,128)S(1)} collective-permute-done((f32[256,128]{1,0:T(8,128)S(1)}, f32[256,128]{1,0:T(8,128)S(1)}, u32[]{:S(2)}, u32[]{:S(2)}) %collective-permute-start.26) | collective-permute-done | bytes 131104 | tf_op jit(solution)/shard_map/ppermute | solution.py:40
  82.4 5.1 %collective-permute-start.27 = (f32[256,128]{1,0:T(8,128)S(1)}, f32[256,128]{1,0:T(8,128)S(1)}, u32[]{:S(2)}, u32[]{:S(2)}) collective-permute-start(f32[256,128]{1,0:T(8,128)S(1)} %sum_over_y.2.refs_3_), channel_id=1, source_target_pairs={{0,8},{1,9},{2,10},{3,11},{4,12},{5,13},{6,14},{7,15},{8,0},{9,1},... | collective-permute-start | bytes 393224 | tf_op jit(solution)/shard_map/ppermute | solution.py:40
  87.5 2.2 %collective-permute-start.22 = (f32[256,128]{1,0:T(8,128)S(1)}, f32[256,128]{1,0:T(8,128)S(1)}, u32[]{:S(2)}, u32[]{:S(2)}) collective-permute-start(f32[256,128]{1,0:T(8,128)S(1)} %get-tuple-element.56), channel_id=1, source_target_pairs={{0,4},{1,5},{2,6},{3,7},{4,0},{5,1},{6,2},{7,3},{8,12},{9,13},{10,... | collective-permute-start | bytes 393224 | tf_op jit(solution)/shard_map/ppermute | solution.py:40
  89.7 2.5 %collective-permute-start.23 = (f32[256,128]{1,0:T(8,128)S(1)}, f32[256,128]{1,0:T(8,128)S(1)}, u32[]{:S(2)}, u32[]{:S(2)}) collective-permute-start(f32[256,128]{1,0:T(8,128)S(1)} %get-tuple-element.57), channel_id=1, source_target_pairs={{0,6},{1,7},{2,4},{3,5},{4,2},{5,3},{6,0},{7,1},{8,14},{9,15},{10,... | collective-permute-start | bytes 393224 | tf_op jit(solution)/shard_map/ppermute | solution.py:40
  92.2 4.4 %cross.4 = (bf16[2048,512]{1,0:T(8,128)(2,1)S(1)}, bf16[2048,512]{1,0:T(8,128)(2,1)S(1)}, bf16[2048,512]{1,0:T(8,128)(2,1)S(1)}, bf16[2048,512]{1,0:T(8,128)(2,1...) custom-call(bf16[2048,128]{1,0:T(8,128)(2,1)S(1)} %get-tuple-element.50.hot, ...), custom_call_target="tpu_custom_call" | custom-call | flops 1 | bytes 1 | tf_op jit(solution)/shard_map/cross/pallas_call | solution.py:377
  97.8 2.1 %collective-permute-start.28 = (f32[256,128]{1,0:T(8,128)S(1)}, f32[256,128]{1,0:T(8,128)S(1)}, u32[]{:S(2)}, u32[]{:S(2)}) collective-permute-start(f32[256,128]{1,0:T(8,128)S(1)} %get-tuple-element.63.refs_2_.refs_0_), channel_id=1, source_target_pairs={{0,8},{1,9},{2,10},{3,11},{4,12},{5,13},{6,14},{7,15},{8,0},{9,1},... | collective-permute-start | bytes 393224 | tf_op jit(solution)/shard_map/ppermute | solution.py:40
  99.9 2.8 %collective-permute-start.32 = (f32[256,128]{1,0:T(8,128)S(1)}, f32[256,128]{1,0:T(8,128)S(1)}, u32[]{:S(2)}, u32[]{:S(2)}) collective-permute-start(f32[256,128]{1,0:T(8,128)S(1)} %get-tuple-element.63.refs_2_.refs_0_), channel_id=1, source_target_pairs={{0,4},{1,5},{2,6},{3,7},{4,0},{5,1},{6,2},{7,3},{8,12},{9,13},{10,... | collective-permute-start | bytes 393224 | tf_op jit(solution)/shard_map/ppermute | solution.py:40
  102.7 1.9 %collective-permute-start.33 = (f32[256,128]{1,0:T(8,128)S(1)}, f32[256,128]{1,0:T(8,128)S(1)}, u32[]{:S(2)}, u32[]{:S(2)}) collective-permute-start(f32[256,128]{1,0:T(8,128)S(1)} %get-tuple-element.63.refs_2_.refs_0_), channel_id=1, source_target_pairs={{0,6},{1,7},{2,4},{3,5},{4,2},{5,3},{6,0},{7,1},{8,14},{9,15},{10,... | collective-permute-start | bytes 393224 | tf_op jit(solution)/shard_map/ppermute | solution.py:40
  104.6 2.9 %cross.5 = (bf16[2048,512]{1,0:T(8,128)(2,1)S(1)}, bf16[2048,512]{1,0:T(8,128)(2,1)S(1)}, bf16[2048,512]{1,0:T(8,128)(2,1)S(1)}, bf16[2048,512]{1,0:T(8,128)(2,1)S(1)}) custom-call(bf16[2048,128]{1,0:T(8,128)(2,1)S(1)} %get-tuple-element.50.hot, f32[128,128]{1,0:T(8,128)S(1)} %get-tuple-element.51.lengths, f32[2,136,256]{2,1,0:T(8,128)S(1)} %stack.20.near1.refs_0_, ...), custom_call_target="tpu_custom_call" | custom-call | flops 1 | bytes 1 | tf_op jit(solution)/shard_map/cross/pallas_call | solution.py:377
  107.6 1.6 %collective-permute-done.28.refs_4_.refs_0_ = f32[256,128]{1,0:T(8,128)S(1)} collective-permute-done((f32[256,128]{1,0:T(8,128)S(1)}, f32[256,128]{1,0:T(8,128)S(1)}, u32[]{:S(2)}, u32[]{:S(2)}) %collective-permute-start.28) | collective-permute-done | bytes 131104 | tf_op jit(solution)/shard_map/ppermute | solution.py:40
  109.5 3.9 %collective-permute-start.29 = (f32[256,128]{1,0:T(8,128)S(1)}, f32[256,128]{1,0:T(8,128)S(1)}, u32[]{:S(2)}, u32[]{:S(2)}) collective-permute-start(f32[256,128]{1,0:T(8,128)S(1)} %collective-permute-done.28.refs_4_.refs_0_), channel_id=1, source_target_pairs={{0,4},{1,5},{2,6},{3,7},{4,0},{5,1},{6,2},{7,3},{8,12},{9,13},{10,... | collective-permute-start | bytes 393224 | tf_op jit(solution)/shard_map/ppermute | solution.py:40
  114.2 2.9 %predict.7.refs_0_.refs_2_ = f32[2048,128]{1,0:T(8,128)S(1)} custom-call(f32[4,256,128]{2,1,0:T(8,128)S(1)} %stack.21.near, f32[4,256,128]{2,1,0:T(8,128)S(1)} %collective-permute-done.34.other, bf16[2048,512]{1,0:T(8,128)(2,1)S(1)} %get-tuple-element.52.refs_0_.h0, bf16[2048,512]{1,0:T(8,128)(2,1)S(1)} %get-tuple-element.69.l0, ...), custom_call_target="tpu_custom_call" | custom-call | flops 1 | bytes 1 | tf_op jit(solution)/shard_map/predict/pallas_call | solution.py:414
  117.2 2.9 %predict.8.refs_2_.refs_0_ = f32[2048,128]{1,0:T(8,128)S(1)} custom-call(f32[4,256,128]{2,1,0:T(8,128)S(1)} %stack.21.near, f32[4,256,128]{2,1,0:T(8,128)S(1)} %collective-permute-done.34.other, bf16[2048,512]{1,0:T(8,128)(2,1)S(1)} %get-tuple-element.65.h0, bf16[2048,512]{1,0:T(8,128)(2,1)S(1)} %get-tuple-element.66.l0, ...), custom_call_target="tpu_custom_call" | custom-call | flops 1 | bytes 1 | tf_op jit(solution)/shard_map/predict/pallas_call | solution.py:414
  120.2 2.3 %collective-permute-done.30.refs_1_ = f32[256,128]{1,0:T(8,128)S(1)} collective-permute-done((f32[256,128]{1,0:T(8,128)S(1)}, f32[256,128]{1,0:T(8,128)S(1)}, u32[]{:S(2)}, u32[]{:S(2)}) %collective-permute-start.30) | collective-permute-done | bytes 131104 | tf_op jit(solution)/shard_map/ppermute | solution.py:40
  122.6 2.9 %predict.9.refs_0_ = f32[2048,128]{1,0:T(8,128)S(1)} custom-call(f32[2,256,128]{2,1,0:T(8,128)S(1)} %stack.23.near, f32[2,256,128]{2,1,0:T(8,128)S(1)} %collective-permute-done.37.other, bf16[2048,512]{1,0:T(8,128)(2,1)S(1)} %get-tuple-element.75.h0, bf16[2048,512]{1,0:T(8,128)(2,1)S(1)} %get-tuple-element.76.l0, ...), custom_call_target="tpu_custom_call" | custom-call | flops 1 | bytes 1 | tf_op jit(solution)/shard_map/predict/pallas_call | solution.py:414
  128.8 3.8 %collective-permute-start.38 = (f32[512,128]{1,0:T(8,128)S(1)}, f32[512,128]{1,0:T(8,128)S(1)}, u32[]{:S(2)}, u32[]{:S(2)}) collective-permute-start(f32[512,128]{1,0:T(8,128)S(1)} %predict.10.refs_1_), channel_id=1, source_target_pairs={{0,128},{16,144},{32,160},{48,176},{64,192},{80,208},{96,224},{112... | collective-permute-start | bytes 786440 | tf_op jit(solution)/shard_map/ppermute | solution.py:40
  133.2 4.5 %collective-permute-done.40.d = f32[512,128]{1,0:T(8,128)S(1)} collective-permute-done((f32[512,128]{1,0:T(8,128)S(1)}, f32[512,128]{1,0:T(8,128)S(1)}, u32[]{:S(2)}, u32[]{:S(2)}) %collective-permute-start.40) | collective-permute-done | bytes 262176 | tf_op jit(solution)/shard_map/ppermute | solution.py:40
  137.9 6.6 %collective-permute-done.38.b = f32[512,128]{1,0:T(8,128)S(1)} collective-permute-done((f32[512,128]{1,0:T(8,128)S(1)}, f32[512,128]{1,0:T(8,128)S(1)}, u32[]{:S(2)}, u32[]{:S(2)}) %collective-permute-start.38) | collective-permute-done | bytes 262176 | tf_op jit(solution)/shard_map/ppermute | solution.py:40
  144.7 3.1 %collective-permute-start.42 = (f32[128,128]{1,0:T(8,128)S(1)}, f32[128,128]{1,0:T(8,128)S(1)}, u32[]{:S(2)}, u32[]{:S(2)}) collective-permute-start(f32[128,128]{1,0:T(8,128)S(1)} %get-tuple-element.80), channel_id=1, source_target_pairs={{0,32},{16,48},{32,0},{48,16},{64,96},{80,112},{96,64},{112,80},{1... | collective-permute-start | bytes 196616 | tf_op jit(solution)/shard_map/ppermute | solution.py:40
  149.7 2.1 %collective-permute-done.42.c = f32[128,128]{1,0:T(8,128)S(1)} collective-permute-done((f32[128,128]{1,0:T(8,128)S(1)}, f32[128,128]{1,0:T(8,128)S(1)}, u32[]{:S(2)}, u32[]{:S(2)}) %collective-permute-start.42) | collective-permute-done | bytes 65568 | tf_op jit(solution)/shard_map/ppermute | solution.py:40
  151.8 1.7 %collective-permute-done.43.d = f32[128,128]{1,0:T(8,128)S(1)} collective-permute-done((f32[128,128]{1,0:T(8,128)S(1)}, f32[128,128]{1,0:T(8,128)S(1)}, u32[]{:S(2)}, u32[]{:S(2)}) %collective-permute-start.43) | collective-permute-done | bytes 65568 | tf_op jit(solution)/shard_map/ppermute | solution.py:40
  (85 shorter events, 19.1 us)
Async XLA Ops:
  1.7 14.7 %collective-permute-start = (f32[136,256]{1,0:T(8,128)S(1)}, f32[136,256]{1,0:T(8,128)S(1)}, u32[]{:S(2)}, u32[]{:S(2)}) collective-permute-start(f32[136,256]{1,0:T(8,128)S(1)} %own_observations.1.refs_0_), channel_id=1, source_target_pairs={{0,2},{1,3},{2,0},{3,1},{4,6},{5,7},{6,4},{7,5},{8,10},{9,11},{10,... | collective-permute-start | bytes 417800 | tf_op jit(solution)/shard_map/ppermute | solution.py:40
  3.4 13.0 %collective-permute-start.1 = (f32[136,256]{1,0:T(8,128)S(1)}, f32[136,256]{1,0:T(8,128)S(1)}, u32[]{:S(2)}, u32[]{:S(2)}) collective-permute-start(f32[136,256]{1,0:T(8,128)S(1)} %own_observations.1.refs_0_), channel_id=1, source_target_pairs={{0,4},{1,5},{2,6},{3,7},{4,0},{5,1},{6,2},{7,3},{8,12},{9,13},{10,... | collective-permute-start | bytes 417800 | tf_op jit(solution)/shard_map/ppermute | solution.py:40
  6.3 10.2 %collective-permute-start.2 = (f32[136,256]{1,0:T(8,128)S(1)}, f32[136,256]{1,0:T(8,128)S(1)}, u32[]{:S(2)}, u32[]{:S(2)}) collective-permute-start(f32[136,256]{1,0:T(8,128)S(1)} %own_observations.1.refs_0_), channel_id=1, source_target_pairs={{0,6},{1,7},{2,4},{3,5},{4,2},{5,3},{6,0},{7,1},{8,14},{9,15},{10,... | collective-permute-start | bytes 417800 | tf_op jit(solution)/shard_map/ppermute | solution.py:40
  6.5 12.0 %collective-permute-start.4 = (f32[136,256]{1,0:T(8,128)S(1)}, f32[136,256]{1,0:T(8,128)S(1)}, u32[]{:S(2)}, u32[]{:S(2)}) collective-permute-start(f32[136,256]{1,0:T(8,128)S(1)} %own_observations.1.refs_0_), channel_id=1, source_target_pairs={{0,8},{1,9},{2,10},{3,11},{4,12},{5,13},{6,14},{7,15},{8,0},{9,1},... | collective-permute-start | bytes 417800 | tf_op jit(solution)/shard_map/ppermute | solution.py:40
  16.5 11.6 %collective-permute-start.3 = (f32[4,136,256]{2,1,0:T(8,128)S(1)}, f32[4,136,256]{2,1,0:T(8,128)S(1)}, u32[]{:S(2)}, u32[]{:S(2)}) collective-permute-start(f32[4,136,256]{2,1,0:T(8,128)S(1)} %stack.18.near.refs_0_.refs_2_), channel_id=1, source_target_pairs={{0,1},{1,0},{2,3},{3,2},{4,5},{5,4},{6,7},{7,6},{8,9},{9,8},{10,11... | collective-permute-start | bytes 1671176 | tf_op jit(solution)/shard_map/ppermute | solution.py:40
  18.5 7.9 %collective-permute-start.7 = (f32[136,256]{1,0:T(8,128)S(1)}, f32[136,256]{1,0:T(8,128)S(1)}, u32[]{:S(2)}, u32[]{:S(2)}) collective-permute-start(f32[136,256]{1,0:T(8,128)S(1)} %collective-permute-done.4.refs_0_), channel_id=1, source_target_pairs={{0,4},{1,5},{2,6},{3,7},{4,0},{5,1},{6,2},{7,3},{8,12},{9,13},{10,... | collective-permute-start | bytes 417800 | tf_op jit(solution)/shard_map/ppermute | solution.py:40
  20.5 6.8 %collective-permute-start.8 = (f32[136,256]{1,0:T(8,128)S(1)}, f32[136,256]{1,0:T(8,128)S(1)}, u32[]{:S(2)}, u32[]{:S(2)}) collective-permute-start(f32[136,256]{1,0:T(8,128)S(1)} %collective-permute-done.4.refs_0_), channel_id=1, source_target_pairs={{0,6},{1,7},{2,4},{3,5},{4,2},{5,3},{6,0},{7,1},{8,14},{9,15},{10,... | collective-permute-start | bytes 417800 | tf_op jit(solution)/shard_map/ppermute | solution.py:40
  21.5 6.0 %collective-permute-start.5 = (f32[136,256]{1,0:T(8,128)S(1)}, f32[136,256]{1,0:T(8,128)S(1)}, u32[]{:S(2)}, u32[]{:S(2)}) collective-permute-start(f32[136,256]{1,0:T(8,128)S(1)} %collective-permute-done.4.refs_0_), channel_id=1, source_target_pairs={{0,2},{1,3},{2,0},{3,1},{4,6},{5,7},{6,4},{7,5},{8,10},{9,11},{10,... | collective-permute-start | bytes 417800 | tf_op jit(solution)/shard_map/ppermute | solution.py:40
  27.3 2.5 %collective-permute-start.9 = (f32[2,136,256]{2,1,0:T(8,128)S(1)}, f32[2,136,256]{2,1,0:T(8,128)S(1)}, u32[]{:S(2)}, u32[]{:S(2)}) collective-permute-start(f32[2,136,256]{2,1,0:T(8,128)S(1)} %stack.20.near1.refs_0_), channel_id=1, source_target_pairs={{0,1},{1,0},{2,3},{3,2},{4,5},{5,4},{6,7},{7,6},{8,9},{9,8},{10,11... | collective-permute-start | bytes 835592 | tf_op jit(solution)/shard_map/ppermute | solution.py:40
  27.6 2.2 %collective-permute-start.6 = (f32[2,136,256]{2,1,0:T(8,128)S(1)}, f32[2,136,256]{2,1,0:T(8,128)S(1)}, u32[]{:S(2)}, u32[]{:S(2)}) collective-permute-start(f32[2,136,256]{2,1,0:T(8,128)S(1)} %stack.19.near0.refs_1_), channel_id=1, source_target_pairs={{0,1},{1,0},{2,3},{3,2},{4,5},{5,4},{6,7},{7,6},{8,9},{9,8},{10,11... | collective-permute-start | bytes 835592 | tf_op jit(solution)/shard_map/ppermute | solution.py:40
  28.1 1.8 %copy-start.1 = (s32[2048]{0:T(1024)S(1)}, s32[2048]{0:T(1024)}, u32[]{:S(2)}) copy-start(s32[2048]{0:T(1024)} %param.19) | copy-start | bytes 24580
  29.8 23.0 %copy-start.2 = (f32[512]{0:T(512)S(1)}, f32[512]{0:T(512)}, u32[]{:S(2)}) copy-start(f32[512]{0:T(512)} %param.11) | copy-start | bytes 6148
  29.9 23.0 %copy-start.3 = (f32[128]{0:T(128)S(1)}, f32[128]{0:T(128)}, u32[]{:S(2)}) copy-start(f32[128]{0:T(128)} %param.13) | copy-start | bytes 1540
  29.9 28.5 %copy-start.4 = (f32[10]{0:T(128)S(1)}, f32[10]{0:T(128)}, u32[]{:S(2)}) copy-start(f32[10]{0:T(128)} %length_scales.1) | copy-start | bytes 124
  31.7 4.8 %collective-permute-start.10 = (f32[40,512]{1,0:T(8,128)S(1)}, f32[40,512]{1,0:T(8,128)S(1)}, u32[]{:S(2)}, u32[]{:S(2)}) collective-permute-start(f32[40,512]{1,0:T(8,128)S(1)} %get-tuple-element.45), channel_id=1, source_target_pairs={{0,64},{16,80},{32,96},{48,112},{64,0},{80,16},{96,32},{112,48},{1... | collective-permute-start | bytes 245768 | tf_op jit(solution)/shard_map/ppermute | solution.py:40
  33.2 7.0 %collective-permute-start.11 = (f32[40,512]{1,0:T(8,128)S(1)}, f32[40,512]{1,0:T(8,128)S(1)}, u32[]{:S(2)}, u32[]{:S(2)}) collective-permute-start(f32[40,512]{1,0:T(8,128)S(1)} %get-tuple-element.46), channel_id=1, source_target_pairs={{0,128},{16,144},{32,160},{48,176},{64,192},{80,208},{96,224},{112... | collective-permute-start | bytes 245768 | tf_op jit(solution)/shard_map/ppermute | solution.py:40
  36.0 6.0 %collective-permute-start.12 = (f32[40,512]{1,0:T(8,128)S(1)}, f32[40,512]{1,0:T(8,128)S(1)}, u32[]{:S(2)}, u32[]{:S(2)}) collective-permute-start(f32[40,512]{1,0:T(8,128)S(1)} %get-tuple-element.47), channel_id=1, source_target_pairs={{0,192},{16,208},{32,224},{48,240},{64,128},{80,144},{96,160},{112... | collective-permute-start | bytes 245768 | tf_op jit(solution)/shard_map/ppermute | solution.py:40
  42.0 5.1 %collective-permute-start.13 = (f32[40,512]{1,0:T(8,128)S(1)}, f32[40,512]{1,0:T(8,128)S(1)}, u32[]{:S(2)}, u32[]{:S(2)}) collective-permute-start(f32[40,512]{1,0:T(8,128)S(1)} %sum_over_x.1.own), channel_id=1, source_target_pairs={{0,16},{16,0},{32,48},{48,32},{64,80},{80,64},{96,112},{112,96},{1... | collective-permute-start | bytes 245768 | tf_op jit(solution)/shard_map/ppermute | solution.py:40
  43.1 7.8 %collective-permute-start.14 = (f32[40,512]{1,0:T(8,128)S(1)}, f32[40,512]{1,0:T(8,128)S(1)}, u32[]{:S(2)}, u32[]{:S(2)}) collective-permute-start(f32[40,512]{1,0:T(8,128)S(1)} %sum_over_x.1.own), channel_id=1, source_target_pairs={{0,32},{16,48},{32,0},{48,16},{64,96},{80,112},{96,64},{112,80},{1... | collective-permute-start | bytes 245768 | tf_op jit(solution)/shard_map/ppermute | solution.py:40
  45.6 7.2 %collective-permute-start.15 = (f32[40,512]{1,0:T(8,128)S(1)}, f32[40,512]{1,0:T(8,128)S(1)}, u32[]{:S(2)}, u32[]{:S(2)}) collective-permute-start(f32[40,512]{1,0:T(8,128)S(1)} %sum_over_x.1.own), channel_id=1, source_target_pairs={{0,48},{16,32},{32,16},{48,0},{64,112},{80,96},{96,80},{112,64},{1... | collective-permute-start | bytes 245768 | tf_op jit(solution)/shard_map/ppermute | solution.py:40
  53.5 10.0 %collective-permute-start.16 = (f32[32,512]{1,0:T(8,128)S(1)}, f32[32,512]{1,0:T(8,128)S(1)}, u32[]{:S(2)}, u32[]{:S(2)}) collective-permute-start(f32[32,512]{1,0:T(8,128)S(1)} %get-tuple-element.48.a), channel_id=1, source_target_pairs={{0,64},{16,80},{32,96},{48,112},{64,0},{80,16},{96,32},{112,48},{1... | collective-permute-start | bytes 196616 | tf_op jit(solution)/shard_map/ppermute | solution.py:40
  53.6 9.9 %collective-permute-start.17 = (f32[32,512]{1,0:T(8,128)S(1)}, f32[32,512]{1,0:T(8,128)S(1)}, u32[]{:S(2)}, u32[]{:S(2)}) collective-permute-start(f32[32,512]{1,0:T(8,128)S(1)} %get-tuple-element.48.a), channel_id=1, source_target_pairs={{0,128},{16,144},{32,160},{48,176},{64,192},{80,208},{96,224},{112... | collective-permute-start | bytes 196616 | tf_op jit(solution)/shard_map/ppermute | solution.py:40
  56.3 7.3 %collective-permute-start.18 = (f32[32,512]{1,0:T(8,128)S(1)}, f32[32,512]{1,0:T(8,128)S(1)}, u32[]{:S(2)}, u32[]{:S(2)}) collective-permute-start(f32[32,512]{1,0:T(8,128)S(1)} %get-tuple-element.48.a), channel_id=1, source_target_pairs={{0,192},{16,208},{32,224},{48,240},{64,128},{80,144},{96,160},{112... | collective-permute-start | bytes 196616 | tf_op jit(solution)/shard_map/ppermute | solution.py:40
  65.9 2.0 %collective-permute-start.19 = (f32[4,256,128]{2,1,0:T(8,128)S(1)}, f32[4,256,128]{2,1,0:T(8,128)S(1)}, u32[]{:S(2)}, u32[]{:S(2)}) collective-permute-start(f32[4,256,128]{2,1,0:T(8,128)S(1)} %expand.5), channel_id=1, source_target_pairs={{0,1},{1,0},{2,3},{3,2},{4,5},{5,4},{6,7},{7,6},{8,9},{9,8},{10,11... | collective-permute-start | bytes 1572872 | tf_op jit(solution)/shard_map/ppermute | solution.py:40
  69.3 6.3 %collective-permute-start.20 = (f32[4,256,128]{2,1,0:T(8,128)S(1)}, f32[4,256,128]{2,1,0:T(8,128)S(1)}, u32[]{:S(2)}, u32[]{:S(2)}) collective-permute-start(f32[4,256,128]{2,1,0:T(8,128)S(1)} %expand.7), channel_id=1, source_target_pairs={{0,1},{1,0},{2,3},{3,2},{4,5},{5,4},{6,7},{7,6},{8,9},{9,8},{10,11... | collective-permute-start | bytes 1572872 | tf_op jit(solution)/shard_map/ppermute | solution.py:40
  69.5 6.3 %collective-permute-start.24 = (f32[256,128]{1,0:T(8,128)S(1)}, f32[256,128]{1,0:T(8,128)S(1)}, u32[]{:S(2)}, u32[]{:S(2)}) collective-permute-start(f32[256,128]{1,0:T(8,128)S(1)} %get-tuple-element.58), channel_id=1, source_target_pairs={{0,2},{1,3},{2,0},{3,1},{4,6},{5,7},{6,4},{7,5},{8,10},{9,11},{10,... | collective-permute-start | bytes 393224 | tf_op jit(solution)/shard_map/ppermute | solution.py:40
  69.7 10.2 %collective-permute-start.25 = (f32[256,128]{1,0:T(8,128)S(1)}, f32[256,128]{1,0:T(8,128)S(1)}, u32[]{:S(2)}, u32[]{:S(2)}) collective-permute-start(f32[256,128]{1,0:T(8,128)S(1)} %get-tuple-element.59), channel_id=1, source_target_pairs={{0,4},{1,5},{2,6},{3,7},{4,0},{5,1},{6,2},{7,3},{8,12},{9,13},{10,... | collective-permute-start | bytes 393224 | tf_op jit(solution)/shard_map/ppermute | solution.py:40
  73.3 9.0 %collective-permute-start.26 = (f32[256,128]{1,0:T(8,128)S(1)}, f32[256,128]{1,0:T(8,128)S(1)}, u32[]{:S(2)}, u32[]{:S(2)}) collective-permute-start(f32[256,128]{1,0:T(8,128)S(1)} %get-tuple-element.60), channel_id=1, source_target_pairs={{0,6},{1,7},{2,4},{3,5},{4,2},{5,3},{6,0},{7,1},{8,14},{9,15},{10,... | collective-permute-start | bytes 393224 | tf_op jit(solution)/shard_map/ppermute | solution.py:40
  82.4 14.2 %collective-permute-start.27 = (f32[256,128]{1,0:T(8,128)S(1)}, f32[256,128]{1,0:T(8,128)S(1)}, u32[]{:S(2)}, u32[]{:S(2)}) collective-permute-start(f32[256,128]{1,0:T(8,128)S(1)} %sum_over_y.2.refs_3_), channel_id=1, source_target_pairs={{0,8},{1,9},{2,10},{3,11},{4,12},{5,13},{6,14},{7,15},{8,0},{9,1},... | collective-permute-start | bytes 393224 | tf_op jit(solution)/shard_map/ppermute | solution.py:40
  87.5 9.1 %collective-permute-start.21 = (f32[256,128]{1,0:T(8,128)S(1)}, f32[256,128]{1,0:T(8,128)S(1)}, u32[]{:S(2)}, u32[]{:S(2)}) collective-permute-start(f32[256,128]{1,0:T(8,128)S(1)} %get-tuple-element.55), channel_id=1, source_target_pairs={{0,2},{1,3},{2,0},{3,1},{4,6},{5,7},{6,4},{7,5},{8,10},{9,11},{10,... | collective-permute-start | bytes 393224 | tf_op jit(solution)/shard_map/ppermute | solution.py:40
  87.5 9.1 %collective-permute-start.22 = (f32[256,128]{1,0:T(8,128)S(1)}, f32[256,128]{1,0:T(8,128)S(1)}, u32[]{:S(2)}, u32[]{:S(2)}) collective-permute-start(f32[256,128]{1,0:T(8,128)S(1)} %get-tuple-element.56), channel_id=1, source_target_pairs={{0,4},{1,5},{2,6},{3,7},{4,0},{5,1},{6,2},{7,3},{8,12},{9,13},{10,... | collective-permute-start | bytes 393224 | tf_op jit(solution)/shard_map/ppermute | solution.py:40
  89.7 7.5 %collective-permute-start.23 = (f32[256,128]{1,0:T(8,128)S(1)}, f32[256,128]{1,0:T(8,128)S(1)}, u32[]{:S(2)}, u32[]{:S(2)}) collective-permute-start(f32[256,128]{1,0:T(8,128)S(1)} %get-tuple-element.57), channel_id=1, source_target_pairs={{0,6},{1,7},{2,4},{3,5},{4,2},{5,3},{6,0},{7,1},{8,14},{9,15},{10,... | collective-permute-start | bytes 393224 | tf_op jit(solution)/shard_map/ppermute | solution.py:40
  97.8 11.3 %collective-permute-start.28 = (f32[256,128]{1,0:T(8,128)S(1)}, f32[256,128]{1,0:T(8,128)S(1)}, u32[]{:S(2)}, u32[]{:S(2)}) collective-permute-start(f32[256,128]{1,0:T(8,128)S(1)} %get-tuple-element.63.refs_2_.refs_0_), channel_id=1, source_target_pairs={{0,8},{1,9},{2,10},{3,11},{4,12},{5,13},{6,14},{7,15},{8,0},{9,1},... | collective-permute-start | bytes 393224 | tf_op jit(solution)/shard_map/ppermute | solution.py:40
  99.9 9.2 %collective-permute-start.31 = (f32[256,128]{1,0:T(8,128)S(1)}, f32[256,128]{1,0:T(8,128)S(1)}, u32[]{:S(2)}, u32[]{:S(2)}) collective-permute-start(f32[256,128]{1,0:T(8,128)S(1)} %get-tuple-element.63.refs_2_.refs_0_), channel_id=1, source_target_pairs={{0,2},{1,3},{2,0},{3,1},{4,6},{5,7},{6,4},{7,5},{8,10},{9,11},{10,... | collective-permute-start | bytes 393224 | tf_op jit(solution)/shard_map/ppermute | solution.py:40
  99.9 9.2 %collective-permute-start.32 = (f32[256,128]{1,0:T(8,128)S(1)}, f32[256,128]{1,0:T(8,128)S(1)}, u32[]{:S(2)}, u32[]{:S(2)}) collective-permute-start(f32[256,128]{1,0:T(8,128)S(1)} %get-tuple-element.63.refs_2_.refs_0_), channel_id=1, source_target_pairs={{0,4},{1,5},{2,6},{3,7},{4,0},{5,1},{6,2},{7,3},{8,12},{9,13},{10,... | collective-permute-start | bytes 393224 | tf_op jit(solution)/shard_map/ppermute | solution.py:40
  102.7 6.6 %collective-permute-start.33 = (f32[256,128]{1,0:T(8,128)S(1)}, f32[256,128]{1,0:T(8,128)S(1)}, u32[]{:S(2)}, u32[]{:S(2)}) collective-permute-start(f32[256,128]{1,0:T(8,128)S(1)} %get-tuple-element.63.refs_2_.refs_0_), channel_id=1, source_target_pairs={{0,6},{1,7},{2,4},{3,5},{4,2},{5,3},{6,0},{7,1},{8,14},{9,15},{10,... | collective-permute-start | bytes 393224 | tf_op jit(solution)/shard_map/ppermute | solution.py:40
  109.3 4.9 %collective-permute-start.34 = (f32[4,256,128]{2,1,0:T(8,128)S(1)}, f32[4,256,128]{2,1,0:T(8,128)S(1)}, u32[]{:S(2)}, u32[]{:S(2)}) collective-permute-start(f32[4,256,128]{2,1,0:T(8,128)S(1)} %stack.21.near), channel_id=1, source_target_pairs={{0,1},{1,0},{2,3},{3,2},{4,5},{5,4},{6,7},{7,6},{8,9},{9,8},{10,11... | collective-permute-start | bytes 1572872 | tf_op jit(solution)/shard_map/ppermute | solution.py:40
  109.4 7.7 %collective-permute-start.36 = (f32[256,128]{1,0:T(8,128)S(1)}, f32[256,128]{1,0:T(8,128)S(1)}, u32[]{:S(2)}, u32[]{:S(2)}) collective-permute-start(f32[256,128]{1,0:T(8,128)S(1)} %collective-permute-done.28.refs_4_.refs_0_), channel_id=1, source_target_pairs={{0,2},{1,3},{2,0},{3,1},{4,6},{5,7},{6,4},{7,5},{8,10},{9,11},{10,... | collective-permute-start | bytes 393224 | tf_op jit(solution)/shard_map/ppermute | solution.py:40
  109.5 10.7 %collective-permute-start.29 = (f32[256,128]{1,0:T(8,128)S(1)}, f32[256,128]{1,0:T(8,128)S(1)}, u32[]{:S(2)}, u32[]{:S(2)}) collective-permute-start(f32[256,128]{1,0:T(8,128)S(1)} %collective-permute-done.28.refs_4_.refs_0_), channel_id=1, source_target_pairs={{0,4},{1,5},{2,6},{3,7},{4,0},{5,1},{6,2},{7,3},{8,12},{9,13},{10,... | collective-permute-start | bytes 393224 | tf_op jit(solution)/shard_map/ppermute | solution.py:40
  113.4 9.1 %collective-permute-start.30 = (f32[256,128]{1,0:T(8,128)S(1)}, f32[256,128]{1,0:T(8,128)S(1)}, u32[]{:S(2)}, u32[]{:S(2)}) collective-permute-start(f32[256,128]{1,0:T(8,128)S(1)} %collective-permute-done.28.refs_4_.refs_0_), channel_id=1, source_target_pairs={{0,6},{1,7},{2,4},{3,5},{4,2},{5,3},{6,0},{7,1},{8,14},{9,15},{10,... | collective-permute-start | bytes 393224 | tf_op jit(solution)/shard_map/ppermute | solution.py:40
  117.1 5.5 %collective-permute-start.37 = (f32[2,256,128]{2,1,0:T(8,128)S(1)}, f32[2,256,128]{2,1,0:T(8,128)S(1)}, u32[]{:S(2)}, u32[]{:S(2)}) collective-permute-start(f32[2,256,128]{2,1,0:T(8,128)S(1)} %stack.23.near), channel_id=1, source_target_pairs={{0,1},{1,0},{2,3},{3,2},{4,5},{5,4},{6,7},{7,6},{8,9},{9,8},{10,11... | collective-permute-start | bytes 786440 | tf_op jit(solution)/shard_map/ppermute | solution.py:40
  122.5 3.0 %collective-permute-start.35 = (f32[2,256,128]{2,1,0:T(8,128)S(1)}, f32[2,256,128]{2,1,0:T(8,128)S(1)}, u32[]{:S(2)}, u32[]{:S(2)}) collective-permute-start(f32[2,256,128]{2,1,0:T(8,128)S(1)} %stack.22.near), channel_id=1, source_target_pairs={{0,1},{1,0},{2,3},{3,2},{4,5},{5,4},{6,7},{7,6},{8,9},{9,8},{10,11... | collective-permute-start | bytes 786440 | tf_op jit(solution)/shard_map/ppermute | solution.py:40
  127.7 10.0 %collective-permute-start.40 = (f32[512,128]{1,0:T(8,128)S(1)}, f32[512,128]{1,0:T(8,128)S(1)}, u32[]{:S(2)}, u32[]{:S(2)}) collective-permute-start(f32[512,128]{1,0:T(8,128)S(1)} %predict.12.refs_1_), channel_id=1, source_target_pairs={{0,192},{16,208},{32,224},{48,240},{64,128},{80,144},{96,160},{112... | collective-permute-start | bytes 786440 | tf_op jit(solution)/shard_map/ppermute | solution.py:40
  128.8 9.1 %collective-permute-start.39 = (f32[512,128]{1,0:T(8,128)S(1)}, f32[512,128]{1,0:T(8,128)S(1)}, u32[]{:S(2)}, u32[]{:S(2)}) collective-permute-start(f32[512,128]{1,0:T(8,128)S(1)} %predict.11.refs_1_), channel_id=1, source_target_pairs={{0,64},{16,80},{32,96},{48,112},{64,0},{80,16},{96,32},{112,48},{1... | collective-permute-start | bytes 786440 | tf_op jit(solution)/shard_map/ppermute | solution.py:40
  128.8 15.8 %collective-permute-start.38 = (f32[512,128]{1,0:T(8,128)S(1)}, f32[512,128]{1,0:T(8,128)S(1)}, u32[]{:S(2)}, u32[]{:S(2)}) collective-permute-start(f32[512,128]{1,0:T(8,128)S(1)} %predict.10.refs_1_), channel_id=1, source_target_pairs={{0,128},{16,144},{32,160},{48,176},{64,192},{80,208},{96,224},{112... | collective-permute-start | bytes 786440 | tf_op jit(solution)/shard_map/ppermute | solution.py:40
  144.6 5.1 %collective-permute-start.41 = (f32[128,128]{1,0:T(8,128)S(1)}, f32[128,128]{1,0:T(8,128)S(1)}, u32[]{:S(2)}, u32[]{:S(2)}) collective-permute-start(f32[128,128]{1,0:T(8,128)S(1)} %get-tuple-element.79), channel_id=1, source_target_pairs={{0,16},{16,0},{32,48},{48,32},{64,80},{80,64},{96,112},{112,96},{1... | collective-permute-start | bytes 196616 | tf_op jit(solution)/shard_map/ppermute | solution.py:40
  144.7 7.1 %collective-permute-start.42 = (f32[128,128]{1,0:T(8,128)S(1)}, f32[128,128]{1,0:T(8,128)S(1)}, u32[]{:S(2)}, u32[]{:S(2)}) collective-permute-start(f32[128,128]{1,0:T(8,128)S(1)} %get-tuple-element.80), channel_id=1, source_target_pairs={{0,32},{16,48},{32,0},{48,16},{64,96},{80,112},{96,64},{112,80},{1... | collective-permute-start | bytes 196616 | tf_op jit(solution)/shard_map/ppermute | solution.py:40
  147.8 5.6 %collective-permute-start.43 = (f32[128,128]{1,0:T(8,128)S(1)}, f32[128,128]{1,0:T(8,128)S(1)}, u32[]{:S(2)}, u32[]{:S(2)}) collective-permute-start(f32[128,128]{1,0:T(8,128)S(1)} %get-tuple-element.81), channel_id=1, source_target_pairs={{0,48},{16,32},{32,16},{48,0},{64,112},{80,96},{96,80},{112,64},{1... | collective-permute-start | bytes 196616 | tf_op jit(solution)/shard_map/ppermute | solution.py:40
  (1 other events, 1.8 us)
where the time goes:
time: 155 us; the launch traced here: 154 us
  starting transfers between devices  63.8 us (41%)
  waiting for transfers between devices  46.7 us (30%)
  Pallas kernels  41.5 us (27%)
  between operations  2.41 us (2%)
    ppermute x44, starting transfers between devices, swap(): return lax.ppermute(value, axis, [(i, i ^ bits) for i in range(16)])  63.8 us
    ppermute x44, waiting for transfers between devices, swap(): return lax.ppermute(value, axis, [(i, i ^ bits) for i in range(16)])  46.7 us
    pallas_call x3, Pallas kernels, cross_halves(): pl.pallas_call(functools.partial(cross_kernel, firsts), in_specs=here(2 +...  11.7 us
    pallas_call x7, Pallas kernels, predict(): pl.pallas_call(functools.partial(predict_kernel, first, near_first, total...  11.6 us
    pallas_call x4, Pallas kernels, expand(): pl.pallas_call(functools.partial(expand_kernel, core, far), in_specs=scal...  5.58 us
    pallas_call x1, Pallas kernels, halves(): pl.pallas_call(halves_kernel, in_specs=anywhere(1), out_specs=here(2), ou...  3.61 us
  transfers between devices with their start and end apart: 44, of which 23 were waited for; matrix products, arithmetic and copies ran while one was open for 0% of the time, Pallas kernels for 20%

commit v1 on v0

--- a/solution.py
+++ b/solution.py
@@ -423,16 +423,31 @@
     )(near, other, *cross0, *cross1, *extra, *after)
 
 
-def quarter_kernel(a, b, c, d, *outs):
+def two_kernel(a, b, out):
+    out[...] = a[...] + b[...]
+
+
+def sum_two(a, b):
+    return pl.pallas_call(
+        two_kernel,
+        in_specs=here(2),
+        out_specs=here(1)[0],
+        out_shape=struct(a.shape),
+        compiler_params=params(3),
+        name="sum_two",
+    )(a, b)
+
+
+def quarter_kernel(a, b, c, *outs):
     for g in range(4):
         rows = pl.ds(g * 128, 128)
-        outs[g][...] = (a[rows, :] + b[rows, :]) + (c[rows, :] + d[rows, :])
+        outs[g][...] = a[rows, :] + (b[rows, :] + c[rows, :])
 
 
 def sum_quarters(blocks):
     return pl.pallas_call(
         quarter_kernel,
-        in_specs=here(4),
+        in_specs=here(3),
         out_specs=here(4),
         out_shape=[struct((128, 128))] * 4,
         compiler_params=params(3),
@@ -474,10 +489,10 @@
 
     own = own_block(where, observations, train_codes)
     high, low = halves(basis)
-    near = stack([own] + [swap(own, "narrow", 2 * d) for d in (1, 2, 3)], [high])
+    mirror = swap(own, "narrow", 8)
+    near = stack([own] + [swap(own, "narrow", 2 * d) for d in (1, 2, 3)], [high, mirror])
     other = swap(near, "narrow", 1)
     before = project_near(where, high, low, near, other)
-    mirror = swap(own, "narrow", 8)
     far = [mirror] + [swap(mirror, "narrow", 2 * d) for d in (1, 2, 3)]
     pairs = []
     for pair in (stack(far[:2], []), stack(far[2:], [])):
@@ -490,7 +505,7 @@
 
     hot, lengths = onehot(length_scales, codes)
     sources = [(near, 0), (other, 0), (near, 2), (other, 2)] + [(array, 0) for array in pairs]
-    crosses = cross_halves(hot, lengths, sources[:3], [])
+    crosses = cross_halves(hot, lengths, sources[:2], [])
     wide = rotate_back(where, task_basis, quarters, [crosses[0][0]])
     odd = expand(1, 1, where, high, low, wide, [])
     even = expand(0, 1, where, high, low, wide, [])
@@ -501,12 +516,12 @@
     total = [sums[0]] + [swap(sums[d], "narrow", 2 * d) for d in (1, 2, 3)]
     total = sum_blocks(total, [later[0]])[0]
     mirror = swap(total, "narrow", 8)
-    crosses += cross_halves(hot, lengths, sources[3:6], [total])
+    crosses += cross_halves(hot, lengths, sources[2:5], [total])
     total = [later[0]] + [swap(later[d], "narrow", 2 * d) for d in (1, 2, 3)]
-    block, coefficients = sum_blocks(total + [mirror], [crosses[5][0]], 2)
+    block, coefficients = sum_blocks(total + [mirror], [crosses[4][0]], 2)
 
     mirror = swap(block, "narrow", 8)
-    crosses += cross_halves(hot, lengths, sources[6:], [block])
+    crosses += cross_halves(hot, lengths, sources[5:], [block])
     near = stack([block] + [swap(block, "narrow", 2 * d) for d in (1, 2, 3)], [mirror, crosses[6][0]])
     other = swap(near, "narrow", 1)
     start = predict(near, other, 0, *crosses[0:2], None, 0, 2048)
@@ -518,11 +533,9 @@
     means = predict(near, other, 0, *crosses[4:6], means, 0, 2048)
     near = stack(far[2:], after)
     other = swap(near, "narrow", 1)
-    last, after = {}, []
-    for g in (2, 1, 3, 0):
-        last[g] = predict(near, other, 0, *crosses[6:8], means, g * 512, 512, after)
-        after = [last[g]]
-    quarters = sum_quarters([last[0]] + [swap(last[g], "wide", 4 * g) for g in (2, 1, 3)])
+    last = {g: predict(near, other, 0, *crosses[6:8], means, g * 512, 512) for g in (2, 1, 3, 0)}
+    begun = sum_two(last[0], swap(last[2], "wide", 8))
+    quarters = sum_quarters([begun] + [swap(last[g], "wide", 4 * g) for g in (1, 3)])
     ends = [quarters[0]] + [swap(quarters[g], "wide", g) for g in (1, 2, 3)]
     return coefficients, finish(signal, ends, task_basis, task_values[None])
 

time: 155 us -> 153 us (0.987)
  transfers between devices with their start and end apart: 44 -> 44, of which waited for: 23 -> 21; matrix products, arithmetic and copies ran while one was open for 0% -> 0% of each run, Pallas kernels for 20% -> 21%
where the time goes in v1:
time: 153 us
  starting transfers between devices  62.5 us (41%)
  waiting for transfers between devices  46.5 us (30%)
  Pallas kernels  41.5 us (27%)
  between operations  2.42 us (2%)
    ppermute x44, starting transfers between devices, swap(): return lax.ppermute(value, axis, [(i, i ^ bits) for i in range(16)])  62.5 us
    ppermute x44, waiting for transfers between devices, swap(): return lax.ppermute(value, axis, [(i, i ^ bits) for i in range(16)])  46.5 us
    pallas_call x3, Pallas kernels, cross_halves(): pl.pallas_call(functools.partial(cross_kernel, firsts), in_specs=here(2 +...  11.7 us
    pallas_call x7, Pallas kernels, predict(): pl.pallas_call(functools.partial(predict_kernel, first, near_first, total...  11.6 us
    pallas_call x4, Pallas kernels, expand(): pl.pallas_call(functools.partial(expand_kernel, core, far), in_specs=scal...  5.58 us
    pallas_call x1, Pallas kernels, halves(): pl.pallas_call(halves_kernel, in_specs=anywhere(1), out_specs=here(2), ou...  3.61 us
  transfers between devices with their start and end apart: 44, of which 21 were waited for; matrix products, arithmetic and copies ran while one was open for 0% of the time, Pallas kernels for 21%

profile of v1, /device:TPU:32, one launch (start us, length us, event | category | flops | bytes accessed | tf_op | source)
XLA Modules:
  0.0 153.1 jit_solution(18311806895090835063)
XLA Ops:
  1.7 6.4 %collective-permute-start.3 = (f32[136,256]{1,0:T(8,128)S(1)}, f32[136,256]{1,0:T(8,128)S(1)}, u32[]{:S(2)}, u32[]{:S(2)}) collective-permute-start(f32[136,256]{1,0:T(8,128)S(1)} %own_observations.1.refs_0_), channel_id=1, source_target_pairs={{0,8},{1,9},{2,10},{3,11},{4,12},{5,13},{6,14},{7,15},{8,0},{9,1},... | collective-permute-start | bytes 417800 | tf_op jit(solution)/shard_map/ppermute | solution.py:40
  8.1 1.6 %collective-permute-start = (f32[136,256]{1,0:T(8,128)S(1)}, f32[136,256]{1,0:T(8,128)S(1)}, u32[]{:S(2)}, u32[]{:S(2)}) collective-permute-start(f32[136,256]{1,0:T(8,128)S(1)} %own_observations.1.refs_0_), channel_id=1, source_target_pairs={{0,2},{1,3},{2,0},{3,1},{4,6},{5,7},{6,4},{7,5},{8,10},{9,11},{10,... | collective-permute-start | bytes 417800 | tf_op jit(solution)/shard_map/ppermute | solution.py:40
  9.7 2.9 %collective-permute-start.1 = (f32[136,256]{1,0:T(8,128)S(1)}, f32[136,256]{1,0:T(8,128)S(1)}, u32[]{:S(2)}, u32[]{:S(2)}) collective-permute-start(f32[136,256]{1,0:T(8,128)S(1)} %own_observations.1.refs_0_), channel_id=1, source_target_pairs={{0,4},{1,5},{2,6},{3,7},{4,0},{5,1},{6,2},{7,3},{8,12},{9,13},{10,... | collective-permute-start | bytes 417800 | tf_op jit(solution)/shard_map/ppermute | solution.py:40
  12.8 3.6 %basis_halves.1 = (bf16[4096,512]{1,0:T(8,128)(2,1)S(1)}, bf16[4096,512]{1,0:T(8,128)(2,1)S(1)}) custom-call(f32[4096,512]{1,0:T(8,128)} %basis.1), custom_call_target="tpu_custom_call" | custom-call | flops 1 | bytes 1 | tf_op jit(solution)/shard_map/basis_halves/pallas_call | solution.py:91
  16.4 2.3 %collective-permute-done.1.refs_2_ = f32[136,256]{1,0:T(8,128)S(1)} collective-permute-done((f32[136,256]{1,0:T(8,128)S(1)}, f32[136,256]{1,0:T(8,128)S(1)}, u32[]{:S(2)}, u32[]{:S(2)}) %collective-permute-start.1) | collective-permute-done | bytes 139296 | tf_op jit(solution)/shard_map/ppermute | solution.py:40
  18.8 2.0 %collective-permute-done.2.refs_3_ = f32[136,256]{1,0:T(8,128)S(1)} collective-permute-done((f32[136,256]{1,0:T(8,128)S(1)}, f32[136,256]{1,0:T(8,128)S(1)}, u32[]{:S(2)}, u32[]{:S(2)}) %collective-permute-start.2) | collective-permute-done | bytes 139296 | tf_op jit(solution)/shard_map/ppermute | solution.py:40
  21.0 2.2 %collective-permute-start.8 = (f32[136,256]{1,0:T(8,128)S(1)}, f32[136,256]{1,0:T(8,128)S(1)}, u32[]{:S(2)}, u32[]{:S(2)}) collective-permute-start(f32[136,256]{1,0:T(8,128)S(1)} %collective-permute-done.3.refs_5_.refs_0_), channel_id=1, source_target_pairs={{0,6},{1,7},{2,4},{3,5},{4,2},{5,3},{6,0},{7,1},{8,14},{9,15},{10,... | collective-permute-start | bytes 417800 | tf_op jit(solution)/shard_map/ppermute | solution.py:40
  24.5 4.5 %collective-permute-done.7.refs_0_ = f32[136,256]{1,0:T(8,128)S(1)} collective-permute-done((f32[136,256]{1,0:T(8,128)S(1)}, f32[136,256]{1,0:T(8,128)S(1)}, u32[]{:S(2)}, u32[]{:S(2)}) %collective-permute-start.7) | collective-permute-done | bytes 139296 | tf_op jit(solution)/shard_map/ppermute | solution.py:40
  29.0 2.2 %collective-permute-done.8.refs_1_ = f32[136,256]{1,0:T(8,128)S(1)} collective-permute-done((f32[136,256]{1,0:T(8,128)S(1)}, f32[136,256]{1,0:T(8,128)S(1)}, u32[]{:S(2)}, u32[]{:S(2)}) %collective-permute-start.8) | collective-permute-done | bytes 139296 | tf_op jit(solution)/shard_map/ppermute | solution.py:40
  31.9 1.7 %project_near.1.before = f32[128,512]{1,0:T(8,128)S(1)} custom-call(s32[2]{0:T(128)S(1)} %pad_add_fusion.where, bf16[4096,512]{1,0:T(8,128)(2,1)S(1)} %get-tuple-element.42.refs_4_.high, bf16[4096,512]{1,0:T(8,128)(2,1)S(1)} %get-tuple-element.43.low, f32[4,136,256]{2,1,0:T(8,128)S(1)} %stack.18.near.refs_0_, ...), custom_call_target="tpu_custom_call" | custom-call | flops 1 | bytes 1 | tf_op jit(solution)/shard_map/project_near/pallas_call | solution.py:155
  33.7 1.8 %project.1 = (f32[40,512]{1,0:T(8,128)S(1)}, f32[40,512]{1,0:T(8,128)S(1)}, f32[40,512]{1,0:T(8,128)S(1)}, f32[40,512]{1,0:T(8,128)S(1)}) custom-call(s32[2]{0:T(128)S(1)} %pad_add_fusion.where, bf16[4096,512]{1,0:T(8,128)(2,1)S(1)} %get-tuple-element.42.refs_4_.high, bf16[4096,512]{1,0:T(8,128)(2,1)S(1)} %get-tuple-element.43.low, f32[128,128]{1,0:T(8,128)S(1)} %copy-done, ...), custom_call_target="tpu_custom_call" | custom-call | flops 1 | bytes 1 | tf_op jit(solution)/shard_map/project/pallas_call | solution.py:180
  35.5 1.6 %collective-permute-start.10 = (f32[40,512]{1,0:T(8,128)S(1)}, f32[40,512]{1,0:T(8,128)S(1)}, u32[]{:S(2)}, u32[]{:S(2)}) collective-permute-start(f32[40,512]{1,0:T(8,128)S(1)} %get-tuple-element.45), channel_id=1, source_target_pairs={{0,64},{16,80},{32,96},{48,112},{64,0},{80,16},{96,32},{112,48},{1... | collective-permute-start | bytes 245768 | tf_op jit(solution)/shard_map/ppermute | solution.py:40
  37.1 2.7 %collective-permute-start.11 = (f32[40,512]{1,0:T(8,128)S(1)}, f32[40,512]{1,0:T(8,128)S(1)}, u32[]{:S(2)}, u32[]{:S(2)}) collective-permute-start(f32[40,512]{1,0:T(8,128)S(1)} %get-tuple-element.46), channel_id=1, source_target_pairs={{0,128},{16,144},{32,160},{48,176},{64,192},{80,208},{96,224},{112... | collective-permute-start | bytes 245768 | tf_op jit(solution)/shard_map/ppermute | solution.py:40
  40.3 3.7 %collective-permute-done.11.b = f32[40,512]{1,0:T(8,128)S(1)} collective-permute-done((f32[40,512]{1,0:T(8,128)S(1)}, f32[40,512]{1,0:T(8,128)S(1)}, u32[]{:S(2)}, u32[]{:S(2)}) %collective-permute-start.11) | collective-permute-done | bytes 81952 | tf_op jit(solution)/shard_map/ppermute | solution.py:40
  44.0 1.7 %collective-permute-done.12.c = f32[40,512]{1,0:T(8,128)S(1)} collective-permute-done((f32[40,512]{1,0:T(8,128)S(1)}, f32[40,512]{1,0:T(8,128)S(1)}, u32[]{:S(2)}, u32[]{:S(2)}) %collective-permute-start.12) | collective-permute-done | bytes 81952 | tf_op jit(solution)/shard_map/ppermute | solution.py:40
  46.8 1.5 collective-permute-start.14
  50.8 2.8 %collective-permute-done.14.b = f32[40,512]{1,0:T(8,128)S(1)} collective-permute-done((f32[40,512]{1,0:T(8,128)S(1)}, f32[40,512]{1,0:T(8,128)S(1)}, u32[]{:S(2)}, u32[]{:S(2)}) %collective-permute-start.14) | collective-permute-done | bytes 81952 | tf_op jit(solution)/shard_map/ppermute | solution.py:40
  53.7 2.3 %collective-permute-done.15.c = f32[40,512]{1,0:T(8,128)S(1)} collective-permute-done((f32[40,512]{1,0:T(8,128)S(1)}, f32[40,512]{1,0:T(8,128)S(1)}, u32[]{:S(2)}, u32[]{:S(2)}) %collective-permute-start.15) | collective-permute-done | bytes 81952 | tf_op jit(solution)/shard_map/ppermute | solution.py:40
  56.9 2.6 %collective-permute-start.17 = (f32[32,512]{1,0:T(8,128)S(1)}, f32[32,512]{1,0:T(8,128)S(1)}, u32[]{:S(2)}, u32[]{:S(2)}) collective-permute-start(f32[32,512]{1,0:T(8,128)S(1)} %get-tuple-element.48.a), channel_id=1, source_target_pairs={{0,128},{16,144},{32,160},{48,176},{64,192},{80,208},{96,224},{112... | collective-permute-start | bytes 196616 | tf_op jit(solution)/shard_map/ppermute | solution.py:40
  59.4 2.1 %collective-permute-start.18 = (f32[32,512]{1,0:T(8,128)S(1)}, f32[32,512]{1,0:T(8,128)S(1)}, u32[]{:S(2)}, u32[]{:S(2)}) collective-permute-start(f32[32,512]{1,0:T(8,128)S(1)} %get-tuple-element.48.a), channel_id=1, source_target_pairs={{0,192},{16,208},{32,224},{48,240},{64,128},{80,144},{96,160},{112... | collective-permute-start | bytes 196616 | tf_op jit(solution)/shard_map/ppermute | solution.py:40
  62.3 2.9 %cross.3 = (bf16[2048,512]{1,0:T(8,128)(2,1)S(1)}, bf16[2048,512]{1,0:T(8,128)(2,1)S(1)}, bf16[2048,512]{1,0:T(8,128)(2,1)S(1)}, bf16[2048,512]{1,0:T(8,128)(2,1)S(1)}) custom-call(bf16[2048,128]{1,0:T(8,128)(2,1)S(1)} %get-tuple-element.50.hot, f32[128,128]{1,0:T(8,128)S(1)} %get-tuple-element.51.lengths, f32[4,136,256]{2,1,0:T(8,128)S(1)} %stack.18.near.refs_0_, ...), custom_call_target="tpu_custom_call" | custom-call | flops 1 | bytes 1 | tf_op jit(solution)/shard_map/cross/pallas_call | solution.py:377
  66.2 1.4 expand.5
  67.7 1.4 expand.4.mine
  69.7 1.4 expand.7
  71.3 2.4 %collective-permute-start.25 = (f32[256,128]{1,0:T(8,128)S(1)}, f32[256,128]{1,0:T(8,128)S(1)}, u32[]{:S(2)}, u32[]{:S(2)}) collective-permute-start(f32[256,128]{1,0:T(8,128)S(1)} %get-tuple-element.59), channel_id=1, source_target_pairs={{0,4},{1,5},{2,6},{3,7},{4,0},{5,1},{6,2},{7,3},{8,12},{9,13},{10,... | collective-permute-start | bytes 393224 | tf_op jit(solution)/shard_map/ppermute | solution.py:40
  73.7 2.3 %collective-permute-start.26 = (f32[256,128]{1,0:T(8,128)S(1)}, f32[256,128]{1,0:T(8,128)S(1)}, u32[]{:S(2)}, u32[]{:S(2)}) collective-permute-start(f32[256,128]{1,0:T(8,128)S(1)} %get-tuple-element.60), channel_id=1, source_target_pairs={{0,6},{1,7},{2,4},{3,5},{4,2},{5,3},{6,0},{7,1},{8,14},{9,15},{10,... | collective-permute-start | bytes 393224 | tf_op jit(solution)/shard_map/ppermute | solution.py:40
  77.6 2.7 %collective-permute-done.25.refs_2_ = f32[256,128]{1,0:T(8,128)S(1)} collective-permute-done((f32[256,128]{1,0:T(8,128)S(1)}, f32[256,128]{1,0:T(8,128)S(1)}, u32[]{:S(2)}, u32[]{:S(2)}) %collective-permute-start.25) | collective-permute-done | bytes 131104 | tf_op jit(solution)/shard_map/ppermute | solution.py:40
  80.4 2.4 %collective-permute-done.26.refs_3_ = f32[256,128]{1,0:T(8,128)S(1)} collective-permute-done((f32[256,128]{1,0:T(8,128)S(1)}, f32[256,128]{1,0:T(8,128)S(1)}, u32[]{:S(2)}, u32[]{:S(2)}) %collective-permute-start.26) | collective-permute-done | bytes 131104 | tf_op jit(solution)/shard_map/ppermute | solution.py:40
  82.8 2.1 %collective-permute-start.27 = (f32[256,128]{1,0:T(8,128)S(1)}, f32[256,128]{1,0:T(8,128)S(1)}, u32[]{:S(2)}, u32[]{:S(2)}) collective-permute-start(f32[256,128]{1,0:T(8,128)S(1)} %sum_over_y.2.refs_3_), channel_id=1, source_target_pairs={{0,8},{1,9},{2,10},{3,11},{4,12},{5,13},{6,14},{7,15},{8,0},{9,1},... | collective-permute-start | bytes 393224 | tf_op jit(solution)/shard_map/ppermute | solution.py:40
  84.9 2.6 %collective-permute-start.22 = (f32[256,128]{1,0:T(8,128)S(1)}, f32[256,128]{1,0:T(8,128)S(1)}, u32[]{:S(2)}, u32[]{:S(2)}) collective-permute-start(f32[256,128]{1,0:T(8,128)S(1)} %get-tuple-element.56), channel_id=1, source_target_pairs={{0,4},{1,5},{2,6},{3,7},{4,0},{5,1},{6,2},{7,3},{8,12},{9,13},{10,... | collective-permute-start | bytes 393224 | tf_op jit(solution)/shard_map/ppermute | solution.py:40
  87.5 2.1 %collective-permute-start.23 = (f32[256,128]{1,0:T(8,128)S(1)}, f32[256,128]{1,0:T(8,128)S(1)}, u32[]{:S(2)}, u32[]{:S(2)}) collective-permute-start(f32[256,128]{1,0:T(8,128)S(1)} %get-tuple-element.57), channel_id=1, source_target_pairs={{0,6},{1,7},{2,4},{3,5},{4,2},{5,3},{6,0},{7,1},{8,14},{9,15},{10,... | collective-permute-start | bytes 393224 | tf_op jit(solution)/shard_map/ppermute | solution.py:40
  89.6 4.4 %cross.4 = (bf16[2048,512]{1,0:T(8,128)(2,1)S(1)}, bf16[2048,512]{1,0:T(8,128)(2,1)S(1)}, bf16[2048,512]{1,0:T(8,128)(2,1)S(1)}, bf16[2048,512]{1,0:T(8,128)(2,1...) custom-call(bf16[2048,128]{1,0:T(8,128)(2,1)S(1)} %get-tuple-element.50.hot, ...), custom_call_target="tpu_custom_call" | custom-call | flops 1 | bytes 1 | tf_op jit(solution)/shard_map/cross/pallas_call | solution.py:377
  95.6 5.1 %collective-permute-start.28 = (f32[256,128]{1,0:T(8,128)S(1)}, f32[256,128]{1,0:T(8,128)S(1)}, u32[]{:S(2)}, u32[]{:S(2)}) collective-permute-start(f32[256,128]{1,0:T(8,128)S(1)} %get-tuple-element.63.refs_3_.refs_0_), channel_id=1, source_target_pairs={{0,8},{1,9},{2,10},{3,11},{4,12},{5,13},{6,14},{7,15},{8,0},{9,1},... | collective-permute-start | bytes 393224 | tf_op jit(solution)/shard_map/ppermute | solution.py:40
  100.7 2.4 %collective-permute-start.32 = (f32[256,128]{1,0:T(8,128)S(1)}, f32[256,128]{1,0:T(8,128)S(1)}, u32[]{:S(2)}, u32[]{:S(2)}) collective-permute-start(f32[256,128]{1,0:T(8,128)S(1)} %get-tuple-element.63.refs_3_.refs_0_), channel_id=1, source_target_pairs={{0,4},{1,5},{2,6},{3,7},{4,0},{5,1},{6,2},{7,3},{8,12},{9,13},{10,... | collective-permute-start | bytes 393224 | tf_op jit(solution)/shard_map/ppermute | solution.py:40
  103.1 2.3 %collective-permute-start.33 = (f32[256,128]{1,0:T(8,128)S(1)}, f32[256,128]{1,0:T(8,128)S(1)}, u32[]{:S(2)}, u32[]{:S(2)}) collective-permute-start(f32[256,128]{1,0:T(8,128)S(1)} %get-tuple-element.63.refs_3_.refs_0_), channel_id=1, source_target_pairs={{0,6},{1,7},{2,4},{3,5},{4,2},{5,3},{6,0},{7,1},{8,14},{9,15},{10,... | collective-permute-start | bytes 393224 | tf_op jit(solution)/shard_map/ppermute | solution.py:40
  105.4 4.4 %cross.5 = (bf16[2048,512]{1,0:T(8,128)(2,1)S(1)}, bf16[2048,512]{1,0:T(8,128)(2,1)S(1)}, bf16[2048,512]{1,0:T(8,128)(2,1)S(1)}, bf16[2048,512]{1,0:T(8,128)(2,1...) custom-call(bf16[2048,128]{1,0:T(8,128)(2,1)S(1)} %get-tuple-element.50.hot, ...), custom_call_target="tpu_custom_call" | custom-call | flops 1 | bytes 1 | tf_op jit(solution)/shard_map/cross/pallas_call | solution.py:377
  110.1 3.6 %collective-permute-start.29 = (f32[256,128]{1,0:T(8,128)S(1)}, f32[256,128]{1,0:T(8,128)S(1)}, u32[]{:S(2)}, u32[]{:S(2)}) collective-permute-start(f32[256,128]{1,0:T(8,128)S(1)} %collective-permute-done.28.refs_4_.refs_0_), channel_id=1, source_target_pairs={{0,4},{1,5},{2,6},{3,7},{4,0},{5,1},{6,2},{7,3},{8,12},{9,13},{10,... | collective-permute-start | bytes 393224 | tf_op jit(solution)/shard_map/ppermute | solution.py:40
  114.8 2.9 %predict.7.refs_0_.refs_2_ = f32[2048,128]{1,0:T(8,128)S(1)} custom-call(f32[4,256,128]{2,1,0:T(8,128)S(1)} %stack.21.near, f32[4,256,128]{2,1,0:T(8,128)S(1)} %collective-permute-done.34.other, bf16[2048,512]{1,0:T(8,128)(2,1)S(1)} %get-tuple-element.52.refs_0_.h0, bf16[2048,512]{1,0:T(8,128)(2,1)S(1)} %get-tuple-element.69.l0, ...), custom_call_target="tpu_custom_call" | custom-call | flops 1 | bytes 1 | tf_op jit(solution)/shard_map/predict/pallas_call | solution.py:414
  117.8 2.9 %predict.8.refs_2_.refs_0_ = f32[2048,128]{1,0:T(8,128)S(1)} custom-call(f32[4,256,128]{2,1,0:T(8,128)S(1)} %stack.21.near, f32[4,256,128]{2,1,0:T(8,128)S(1)} %collective-permute-done.34.other, bf16[2048,512]{1,0:T(8,128)(2,1)S(1)} %get-tuple-element.65.h0, bf16[2048,512]{1,0:T(8,128)(2,1)S(1)} %get-tuple-element.66.l0, ...), custom_call_target="tpu_custom_call" | custom-call | flops 1 | bytes 1 | tf_op jit(solution)/shard_map/predict/pallas_call | solution.py:414
  120.7 2.0 %collective-permute-done.30.refs_1_ = f32[256,128]{1,0:T(8,128)S(1)} collective-permute-done((f32[256,128]{1,0:T(8,128)S(1)}, f32[256,128]{1,0:T(8,128)S(1)}, u32[]{:S(2)}, u32[]{:S(2)}) %collective-permute-start.30) | collective-permute-done | bytes 131104 | tf_op jit(solution)/shard_map/ppermute | solution.py:40
  122.9 2.9 %predict.9.refs_0_ = f32[2048,128]{1,0:T(8,128)S(1)} custom-call(f32[2,256,128]{2,1,0:T(8,128)S(1)} %stack.23.near, f32[2,256,128]{2,1,0:T(8,128)S(1)} %collective-permute-done.37.other, bf16[2048,512]{1,0:T(8,128)(2,1)S(1)} %get-tuple-element.61.refs_5_.h0, bf16[2048,512]{1,0:T(8,128)(2,1)S(1)} %get-tuple-element.75.l0, ...), custom_call_target="tpu_custom_call" | custom-call | flops 1 | bytes 1 | tf_op jit(solution)/shard_map/predict/pallas_call | solution.py:414
  127.5 2.0 %collective-permute-start.40 = (f32[512,128]{1,0:T(8,128)S(1)}, f32[512,128]{1,0:T(8,128)S(1)}, u32[]{:S(2)}, u32[]{:S(2)}) collective-permute-start(f32[512,128]{1,0:T(8,128)S(1)} %predict.13), channel_id=1, source_target_pairs={{0,192},{16,208},{32,224},{48,240},{64,128},{80,144},{96,160},{112... | collective-permute-start | bytes 786440 | tf_op jit(solution)/shard_map/ppermute | solution.py:40
  130.2 1.6 %collective-permute-start.39 = (f32[512,128]{1,0:T(8,128)S(1)}, f32[512,128]{1,0:T(8,128)S(1)}, u32[]{:S(2)}, u32[]{:S(2)}) collective-permute-start(f32[512,128]{1,0:T(8,128)S(1)} %predict.12), channel_id=1, source_target_pairs={{0,64},{16,80},{32,96},{48,112},{64,0},{80,16},{96,32},{112,48},{1... | collective-permute-start | bytes 786440 | tf_op jit(solution)/shard_map/ppermute | solution.py:40
  132.5 4.8 %collective-permute-done.38.b = f32[512,128]{1,0:T(8,128)S(1)} collective-permute-done((f32[512,128]{1,0:T(8,128)S(1)}, f32[512,128]{1,0:T(8,128)S(1)}, u32[]{:S(2)}, u32[]{:S(2)}) %collective-permute-start.38) | collective-permute-done | bytes 262176 | tf_op jit(solution)/shard_map/ppermute | solution.py:40
  137.3 5.1 %collective-permute-done.40.c = f32[512,128]{1,0:T(8,128)S(1)} collective-permute-done((f32[512,128]{1,0:T(8,128)S(1)}, f32[512,128]{1,0:T(8,128)S(1)}, u32[]{:S(2)}, u32[]{:S(2)}) %collective-permute-start.40) | collective-permute-done | bytes 262176 | tf_op jit(solution)/shard_map/ppermute | solution.py:40
  143.2 1.9 %collective-permute-start.42 = (f32[128,128]{1,0:T(8,128)S(1)}, f32[128,128]{1,0:T(8,128)S(1)}, u32[]{:S(2)}, u32[]{:S(2)}) collective-permute-start(f32[128,128]{1,0:T(8,128)S(1)} %get-tuple-element.80), channel_id=1, source_target_pairs={{0,32},{16,48},{32,0},{48,16},{64,96},{80,112},{96,64},{112,80},{1... | collective-permute-start | bytes 196616 | tf_op jit(solution)/shard_map/ppermute | solution.py:40
  147.4 2.3 %collective-permute-done.42.c = f32[128,128]{1,0:T(8,128)S(1)} collective-permute-done((f32[128,128]{1,0:T(8,128)S(1)}, f32[128,128]{1,0:T(8,128)S(1)}, u32[]{:S(2)}, u32[]{:S(2)}) %collective-permute-start.42) | collective-permute-done | bytes 65568 | tf_op jit(solution)/shard_map/ppermute | solution.py:40
  149.8 2.3 %collective-permute-done.43.d = f32[128,128]{1,0:T(8,128)S(1)} collective-permute-done((f32[128,128]{1,0:T(8,128)S(1)}, f32[128,128]{1,0:T(8,128)S(1)}, u32[]{:S(2)}, u32[]{:S(2)}) %collective-permute-start.43) | collective-permute-done | bytes 65568 | tf_op jit(solution)/shard_map/ppermute | solution.py:40
  (86 shorter events, 21.9 us)
Async XLA Ops:
  1.7 14.7 %collective-permute-start.3 = (f32[136,256]{1,0:T(8,128)S(1)}, f32[136,256]{1,0:T(8,128)S(1)}, u32[]{:S(2)}, u32[]{:S(2)}) collective-permute-start(f32[136,256]{1,0:T(8,128)S(1)} %own_observations.1.refs_0_), channel_id=1, source_target_pairs={{0,8},{1,9},{2,10},{3,11},{4,12},{5,13},{6,14},{7,15},{8,0},{9,1},... | collective-permute-start | bytes 417800 | tf_op jit(solution)/shard_map/ppermute | solution.py:40
  8.1 8.3 %collective-permute-start = (f32[136,256]{1,0:T(8,128)S(1)}, f32[136,256]{1,0:T(8,128)S(1)}, u32[]{:S(2)}, u32[]{:S(2)}) collective-permute-start(f32[136,256]{1,0:T(8,128)S(1)} %own_observations.1.refs_0_), channel_id=1, source_target_pairs={{0,2},{1,3},{2,0},{3,1},{4,6},{5,7},{6,4},{7,5},{8,10},{9,11},{10,... | collective-permute-start | bytes 417800 | tf_op jit(solution)/shard_map/ppermute | solution.py:40
  9.7 9.1 %collective-permute-start.1 = (f32[136,256]{1,0:T(8,128)S(1)}, f32[136,256]{1,0:T(8,128)S(1)}, u32[]{:S(2)}, u32[]{:S(2)}) collective-permute-start(f32[136,256]{1,0:T(8,128)S(1)} %own_observations.1.refs_0_), channel_id=1, source_target_pairs={{0,4},{1,5},{2,6},{3,7},{4,0},{5,1},{6,2},{7,3},{8,12},{9,13},{10,... | collective-permute-start | bytes 417800 | tf_op jit(solution)/shard_map/ppermute | solution.py:40
  12.6 8.2 %collective-permute-start.2 = (f32[136,256]{1,0:T(8,128)S(1)}, f32[136,256]{1,0:T(8,128)S(1)}, u32[]{:S(2)}, u32[]{:S(2)}) collective-permute-start(f32[136,256]{1,0:T(8,128)S(1)} %own_observations.1.refs_0_), channel_id=1, source_target_pairs={{0,6},{1,7},{2,4},{3,5},{4,2},{5,3},{6,0},{7,1},{8,14},{9,15},{10,... | collective-permute-start | bytes 417800 | tf_op jit(solution)/shard_map/ppermute | solution.py:40
  20.8 11.1 %collective-permute-start.4 = (f32[4,136,256]{2,1,0:T(8,128)S(1)}, f32[4,136,256]{2,1,0:T(8,128)S(1)}, u32[]{:S(2)}, u32[]{:S(2)}) collective-permute-start(f32[4,136,256]{2,1,0:T(8,128)S(1)} %stack.18.near.refs_0_), channel_id=1, source_target_pairs={{0,1},{1,0},{2,3},{3,2},{4,5},{5,4},{6,7},{7,6},{8,9},{9,8},{10,11... | collective-permute-start | bytes 1671176 | tf_op jit(solution)/shard_map/ppermute | solution.py:40
  20.9 8.1 %collective-permute-start.7 = (f32[136,256]{1,0:T(8,128)S(1)}, f32[136,256]{1,0:T(8,128)S(1)}, u32[]{:S(2)}, u32[]{:S(2)}) collective-permute-start(f32[136,256]{1,0:T(8,128)S(1)} %collective-permute-done.3.refs_5_.refs_0_), channel_id=1, source_target_pairs={{0,4},{1,5},{2,6},{3,7},{4,0},{5,1},{6,2},{7,3},{8,12},{9,13},{10,... | collective-permute-start | bytes 417800 | tf_op jit(solution)/shard_map/ppermute | solution.py:40
  21.0 10.2 %collective-permute-start.8 = (f32[136,256]{1,0:T(8,128)S(1)}, f32[136,256]{1,0:T(8,128)S(1)}, u32[]{:S(2)}, u32[]{:S(2)}) collective-permute-start(f32[136,256]{1,0:T(8,128)S(1)} %collective-permute-done.3.refs_5_.refs_0_), channel_id=1, source_target_pairs={{0,6},{1,7},{2,4},{3,5},{4,2},{5,3},{6,0},{7,1},{8,14},{9,15},{10,... | collective-permute-start | bytes 417800 | tf_op jit(solution)/shard_map/ppermute | solution.py:40
  23.2 8.1 %collective-permute-start.5 = (f32[136,256]{1,0:T(8,128)S(1)}, f32[136,256]{1,0:T(8,128)S(1)}, u32[]{:S(2)}, u32[]{:S(2)}) collective-permute-start(f32[136,256]{1,0:T(8,128)S(1)} %collective-permute-done.3.refs_5_.refs_0_), channel_id=1, source_target_pairs={{0,2},{1,3},{2,0},{3,1},{4,6},{5,7},{6,4},{7,5},{8,10},{9,11},{10,... | collective-permute-start | bytes 417800 | tf_op jit(solution)/shard_map/ppermute | solution.py:40
  31.2 2.5 %collective-permute-start.9 = (f32[2,136,256]{2,1,0:T(8,128)S(1)}, f32[2,136,256]{2,1,0:T(8,128)S(1)}, u32[]{:S(2)}, u32[]{:S(2)}) collective-permute-start(f32[2,136,256]{2,1,0:T(8,128)S(1)} %stack.20.near1.refs_1_), channel_id=1, source_target_pairs={{0,1},{1,0},{2,3},{3,2},{4,5},{5,4},{6,7},{7,6},{8,9},{9,8},{10,11... | collective-permute-start | bytes 835592 | tf_op jit(solution)/shard_map/ppermute | solution.py:40
  31.3 2.3 %collective-permute-start.6 = (f32[2,136,256]{2,1,0:T(8,128)S(1)}, f32[2,136,256]{2,1,0:T(8,128)S(1)}, u32[]{:S(2)}, u32[]{:S(2)}) collective-permute-start(f32[2,136,256]{2,1,0:T(8,128)S(1)} %stack.19.near0.refs_2_), channel_id=1, source_target_pairs={{0,1},{1,0},{2,3},{3,2},{4,5},{5,4},{6,7},{7,6},{8,9},{9,8},{10,11... | collective-permute-start | bytes 835592 | tf_op jit(solution)/shard_map/ppermute | solution.py:40
  31.9 1.8 %copy-start.1 = (s32[2048]{0:T(1024)S(1)}, s32[2048]{0:T(1024)}, u32[]{:S(2)}) copy-start(s32[2048]{0:T(1024)} %param.19) | copy-start | bytes 24580
  33.7 22.3 %copy-start.2 = (f32[512]{0:T(512)S(1)}, f32[512]{0:T(512)}, u32[]{:S(2)}) copy-start(f32[512]{0:T(512)} %param.11) | copy-start | bytes 6148
  33.7 22.3 %copy-start.3 = (f32[128]{0:T(128)S(1)}, f32[128]{0:T(128)}, u32[]{:S(2)}) copy-start(f32[128]{0:T(128)} %param.13) | copy-start | bytes 1540
  33.7 27.8 %copy-start.4 = (f32[10]{0:T(128)S(1)}, f32[10]{0:T(128)}, u32[]{:S(2)}) copy-start(f32[10]{0:T(128)} %length_scales.1) | copy-start | bytes 124
  35.5 4.8 %collective-permute-start.10 = (f32[40,512]{1,0:T(8,128)S(1)}, f32[40,512]{1,0:T(8,128)S(1)}, u32[]{:S(2)}, u32[]{:S(2)}) collective-permute-start(f32[40,512]{1,0:T(8,128)S(1)} %get-tuple-element.45), channel_id=1, source_target_pairs={{0,64},{16,80},{32,96},{48,112},{64,0},{80,16},{96,32},{112,48},{1... | collective-permute-start | bytes 245768 | tf_op jit(solution)/shard_map/ppermute | solution.py:40
  37.1 6.9 %collective-permute-start.11 = (f32[40,512]{1,0:T(8,128)S(1)}, f32[40,512]{1,0:T(8,128)S(1)}, u32[]{:S(2)}, u32[]{:S(2)}) collective-permute-start(f32[40,512]{1,0:T(8,128)S(1)} %get-tuple-element.46), channel_id=1, source_target_pairs={{0,128},{16,144},{32,160},{48,176},{64,192},{80,208},{96,224},{112... | collective-permute-start | bytes 245768 | tf_op jit(solution)/shard_map/ppermute | solution.py:40
  39.8 5.9 %collective-permute-start.12 = (f32[40,512]{1,0:T(8,128)S(1)}, f32[40,512]{1,0:T(8,128)S(1)}, u32[]{:S(2)}, u32[]{:S(2)}) collective-permute-start(f32[40,512]{1,0:T(8,128)S(1)} %get-tuple-element.47), channel_id=1, source_target_pairs={{0,192},{16,208},{32,224},{48,240},{64,128},{80,144},{96,160},{112... | collective-permute-start | bytes 245768 | tf_op jit(solution)/shard_map/ppermute | solution.py:40
  45.7 5.1 %collective-permute-start.13 = (f32[40,512]{1,0:T(8,128)S(1)}, f32[40,512]{1,0:T(8,128)S(1)}, u32[]{:S(2)}, u32[]{:S(2)}) collective-permute-start(f32[40,512]{1,0:T(8,128)S(1)} %sum_over_x.1.own), channel_id=1, source_target_pairs={{0,16},{16,0},{32,48},{48,32},{64,80},{80,64},{96,112},{112,96},{1... | collective-permute-start | bytes 245768 | tf_op jit(solution)/shard_map/ppermute | solution.py:40
  46.8 6.8 %collective-permute-start.14 = (f32[40,512]{1,0:T(8,128)S(1)}, f32[40,512]{1,0:T(8,128)S(1)}, u32[]{:S(2)}, u32[]{:S(2)}) collective-permute-start(f32[40,512]{1,0:T(8,128)S(1)} %sum_over_x.1.own), channel_id=1, source_target_pairs={{0,32},{16,48},{32,0},{48,16},{64,96},{80,112},{96,64},{112,80},{1... | collective-permute-start | bytes 245768 | tf_op jit(solution)/shard_map/ppermute | solution.py:40
  48.3 7.7 %collective-permute-start.15 = (f32[40,512]{1,0:T(8,128)S(1)}, f32[40,512]{1,0:T(8,128)S(1)}, u32[]{:S(2)}, u32[]{:S(2)}) collective-permute-start(f32[40,512]{1,0:T(8,128)S(1)} %sum_over_x.1.own), channel_id=1, source_target_pairs={{0,48},{16,32},{32,16},{48,0},{64,112},{80,96},{96,80},{112,64},{1... | collective-permute-start | bytes 245768 | tf_op jit(solution)/shard_map/ppermute | solution.py:40
  56.8 8.5 %collective-permute-start.16 = (f32[32,512]{1,0:T(8,128)S(1)}, f32[32,512]{1,0:T(8,128)S(1)}, u32[]{:S(2)}, u32[]{:S(2)}) collective-permute-start(f32[32,512]{1,0:T(8,128)S(1)} %get-tuple-element.48.a), channel_id=1, source_target_pairs={{0,64},{16,80},{32,96},{48,112},{64,0},{80,16},{96,32},{112,48},{1... | collective-permute-start | bytes 196616 | tf_op jit(solution)/shard_map/ppermute | solution.py:40
  56.9 8.4 %collective-permute-start.17 = (f32[32,512]{1,0:T(8,128)S(1)}, f32[32,512]{1,0:T(8,128)S(1)}, u32[]{:S(2)}, u32[]{:S(2)}) collective-permute-start(f32[32,512]{1,0:T(8,128)S(1)} %get-tuple-element.48.a), channel_id=1, source_target_pairs={{0,128},{16,144},{32,160},{48,176},{64,192},{80,208},{96,224},{112... | collective-permute-start | bytes 196616 | tf_op jit(solution)/shard_map/ppermute | solution.py:40
  59.4 5.9 %collective-permute-start.18 = (f32[32,512]{1,0:T(8,128)S(1)}, f32[32,512]{1,0:T(8,128)S(1)}, u32[]{:S(2)}, u32[]{:S(2)}) collective-permute-start(f32[32,512]{1,0:T(8,128)S(1)} %get-tuple-element.48.a), channel_id=1, source_target_pairs={{0,192},{16,208},{32,224},{48,240},{64,128},{80,144},{96,160},{112... | collective-permute-start | bytes 196616 | tf_op jit(solution)/shard_map/ppermute | solution.py:40
  67.6 2.0 %collective-permute-start.19 = (f32[4,256,128]{2,1,0:T(8,128)S(1)}, f32[4,256,128]{2,1,0:T(8,128)S(1)}, u32[]{:S(2)}, u32[]{:S(2)}) collective-permute-start(f32[4,256,128]{2,1,0:T(8,128)S(1)} %expand.5), channel_id=1, source_target_pairs={{0,1},{1,0},{2,3},{3,2},{4,5},{5,4},{6,7},{7,6},{8,9},{9,8},{10,11... | collective-permute-start | bytes 1572872 | tf_op jit(solution)/shard_map/ppermute | solution.py:40
  71.1 6.3 %collective-permute-start.20 = (f32[4,256,128]{2,1,0:T(8,128)S(1)}, f32[4,256,128]{2,1,0:T(8,128)S(1)}, u32[]{:S(2)}, u32[]{:S(2)}) collective-permute-start(f32[4,256,128]{2,1,0:T(8,128)S(1)} %expand.7), channel_id=1, source_target_pairs={{0,1},{1,0},{2,3},{3,2},{4,5},{5,4},{6,7},{7,6},{8,9},{9,8},{10,11... | collective-permute-start | bytes 1572872 | tf_op jit(solution)/shard_map/ppermute | solution.py:40
  71.3 6.3 %collective-permute-start.24 = (f32[256,128]{1,0:T(8,128)S(1)}, f32[256,128]{1,0:T(8,128)S(1)}, u32[]{:S(2)}, u32[]{:S(2)}) collective-permute-start(f32[256,128]{1,0:T(8,128)S(1)} %get-tuple-element.58), channel_id=1, source_target_pairs={{0,2},{1,3},{2,0},{3,1},{4,6},{5,7},{6,4},{7,5},{8,10},{9,11},{10,... | collective-permute-start | bytes 393224 | tf_op jit(solution)/shard_map/ppermute | solution.py:40
  71.3 9.1 %collective-permute-start.25 = (f32[256,128]{1,0:T(8,128)S(1)}, f32[256,128]{1,0:T(8,128)S(1)}, u32[]{:S(2)}, u32[]{:S(2)}) collective-permute-start(f32[256,128]{1,0:T(8,128)S(1)} %get-tuple-element.59), channel_id=1, source_target_pairs={{0,4},{1,5},{2,6},{3,7},{4,0},{5,1},{6,2},{7,3},{8,12},{9,13},{10,... | collective-permute-start | bytes 393224 | tf_op jit(solution)/shard_map/ppermute | solution.py:40
  73.7 9.0 %collective-permute-start.26 = (f32[256,128]{1,0:T(8,128)S(1)}, f32[256,128]{1,0:T(8,128)S(1)}, u32[]{:S(2)}, u32[]{:S(2)}) collective-permute-start(f32[256,128]{1,0:T(8,128)S(1)} %get-tuple-element.60), channel_id=1, source_target_pairs={{0,6},{1,7},{2,4},{3,5},{4,2},{5,3},{6,0},{7,1},{8,14},{9,15},{10,... | collective-permute-start | bytes 393224 | tf_op jit(solution)/shard_map/ppermute | solution.py:40
  82.8 11.9 %collective-permute-start.27 = (f32[256,128]{1,0:T(8,128)S(1)}, f32[256,128]{1,0:T(8,128)S(1)}, u32[]{:S(2)}, u32[]{:S(2)}) collective-permute-start(f32[256,128]{1,0:T(8,128)S(1)} %sum_over_y.2.refs_3_), channel_id=1, source_target_pairs={{0,8},{1,9},{2,10},{3,11},{4,12},{5,13},{6,14},{7,15},{8,0},{9,1},... | collective-permute-start | bytes 393224 | tf_op jit(solution)/shard_map/ppermute | solution.py:40
  84.9 9.7 %collective-permute-start.21 = (f32[256,128]{1,0:T(8,128)S(1)}, f32[256,128]{1,0:T(8,128)S(1)}, u32[]{:S(2)}, u32[]{:S(2)}) collective-permute-start(f32[256,128]{1,0:T(8,128)S(1)} %get-tuple-element.55), channel_id=1, source_target_pairs={{0,2},{1,3},{2,0},{3,1},{4,6},{5,7},{6,4},{7,5},{8,10},{9,11},{10,... | collective-permute-start | bytes 393224 | tf_op jit(solution)/shard_map/ppermute | solution.py:40
  84.9 9.7 %collective-permute-start.22 = (f32[256,128]{1,0:T(8,128)S(1)}, f32[256,128]{1,0:T(8,128)S(1)}, u32[]{:S(2)}, u32[]{:S(2)}) collective-permute-start(f32[256,128]{1,0:T(8,128)S(1)} %get-tuple-element.56), channel_id=1, source_target_pairs={{0,4},{1,5},{2,6},{3,7},{4,0},{5,1},{6,2},{7,3},{8,12},{9,13},{10,... | collective-permute-start | bytes 393224 | tf_op jit(solution)/shard_map/ppermute | solution.py:40
  87.5 7.5 %collective-permute-start.23 = (f32[256,128]{1,0:T(8,128)S(1)}, f32[256,128]{1,0:T(8,128)S(1)}, u32[]{:S(2)}, u32[]{:S(2)}) collective-permute-start(f32[256,128]{1,0:T(8,128)S(1)} %get-tuple-element.57), channel_id=1, source_target_pairs={{0,6},{1,7},{2,4},{3,5},{4,2},{5,3},{6,0},{7,1},{8,14},{9,15},{10,... | collective-permute-start | bytes 393224 | tf_op jit(solution)/shard_map/ppermute | solution.py:40
  95.6 14.2 %collective-permute-start.28 = (f32[256,128]{1,0:T(8,128)S(1)}, f32[256,128]{1,0:T(8,128)S(1)}, u32[]{:S(2)}, u32[]{:S(2)}) collective-permute-start(f32[256,128]{1,0:T(8,128)S(1)} %get-tuple-element.63.refs_3_.refs_0_), channel_id=1, source_target_pairs={{0,8},{1,9},{2,10},{3,11},{4,12},{5,13},{6,14},{7,15},{8,0},{9,1},... | collective-permute-start | bytes 393224 | tf_op jit(solution)/shard_map/ppermute | solution.py:40
  100.7 9.1 %collective-permute-start.31 = (f32[256,128]{1,0:T(8,128)S(1)}, f32[256,128]{1,0:T(8,128)S(1)}, u32[]{:S(2)}, u32[]{:S(2)}) collective-permute-start(f32[256,128]{1,0:T(8,128)S(1)} %get-tuple-element.63.refs_3_.refs_0_), channel_id=1, source_target_pairs={{0,2},{1,3},{2,0},{3,1},{4,6},{5,7},{6,4},{7,5},{8,10},{9,11},{10,... | collective-permute-start | bytes 393224 | tf_op jit(solution)/shard_map/ppermute | solution.py:40
  100.7 9.1 %collective-permute-start.32 = (f32[256,128]{1,0:T(8,128)S(1)}, f32[256,128]{1,0:T(8,128)S(1)}, u32[]{:S(2)}, u32[]{:S(2)}) collective-permute-start(f32[256,128]{1,0:T(8,128)S(1)} %get-tuple-element.63.refs_3_.refs_0_), channel_id=1, source_target_pairs={{0,4},{1,5},{2,6},{3,7},{4,0},{5,1},{6,2},{7,3},{8,12},{9,13},{10,... | collective-permute-start | bytes 393224 | tf_op jit(solution)/shard_map/ppermute | solution.py:40
  103.1 6.7 %collective-permute-start.33 = (f32[256,128]{1,0:T(8,128)S(1)}, f32[256,128]{1,0:T(8,128)S(1)}, u32[]{:S(2)}, u32[]{:S(2)}) collective-permute-start(f32[256,128]{1,0:T(8,128)S(1)} %get-tuple-element.63.refs_3_.refs_0_), channel_id=1, source_target_pairs={{0,6},{1,7},{2,4},{3,5},{4,2},{5,3},{6,0},{7,1},{8,14},{9,15},{10,... | collective-permute-start | bytes 393224 | tf_op jit(solution)/shard_map/ppermute | solution.py:40
  109.9 4.9 %collective-permute-start.34 = (f32[4,256,128]{2,1,0:T(8,128)S(1)}, f32[4,256,128]{2,1,0:T(8,128)S(1)}, u32[]{:S(2)}, u32[]{:S(2)}) collective-permute-start(f32[4,256,128]{2,1,0:T(8,128)S(1)} %stack.21.near), channel_id=1, source_target_pairs={{0,1},{1,0},{2,3},{3,2},{4,5},{5,4},{6,7},{7,6},{8,9},{9,8},{10,11... | collective-permute-start | bytes 1572872 | tf_op jit(solution)/shard_map/ppermute | solution.py:40
  110.0 7.7 %collective-permute-start.36 = (f32[256,128]{1,0:T(8,128)S(1)}, f32[256,128]{1,0:T(8,128)S(1)}, u32[]{:S(2)}, u32[]{:S(2)}) collective-permute-start(f32[256,128]{1,0:T(8,128)S(1)} %collective-permute-done.28.refs_4_.refs_0_), channel_id=1, source_target_pairs={{0,2},{1,3},{2,0},{3,1},{4,6},{5,7},{6,4},{7,5},{8,10},{9,11},{10,... | collective-permute-start | bytes 393224 | tf_op jit(solution)/shard_map/ppermute | solution.py:40
  110.1 10.7 %collective-permute-start.29 = (f32[256,128]{1,0:T(8,128)S(1)}, f32[256,128]{1,0:T(8,128)S(1)}, u32[]{:S(2)}, u32[]{:S(2)}) collective-permute-start(f32[256,128]{1,0:T(8,128)S(1)} %collective-permute-done.28.refs_4_.refs_0_), channel_id=1, source_target_pairs={{0,4},{1,5},{2,6},{3,7},{4,0},{5,1},{6,2},{7,3},{8,12},{9,13},{10,... | collective-permute-start | bytes 393224 | tf_op jit(solution)/shard_map/ppermute | solution.py:40
  113.7 9.1 %collective-permute-start.30 = (f32[256,128]{1,0:T(8,128)S(1)}, f32[256,128]{1,0:T(8,128)S(1)}, u32[]{:S(2)}, u32[]{:S(2)}) collective-permute-start(f32[256,128]{1,0:T(8,128)S(1)} %collective-permute-done.28.refs_4_.refs_0_), channel_id=1, source_target_pairs={{0,6},{1,7},{2,4},{3,5},{4,2},{5,3},{6,0},{7,1},{8,14},{9,15},{10,... | collective-permute-start | bytes 393224 | tf_op jit(solution)/shard_map/ppermute | solution.py:40
  117.7 5.2 %collective-permute-start.37 = (f32[2,256,128]{2,1,0:T(8,128)S(1)}, f32[2,256,128]{2,1,0:T(8,128)S(1)}, u32[]{:S(2)}, u32[]{:S(2)}) collective-permute-start(f32[2,256,128]{2,1,0:T(8,128)S(1)} %stack.23.near), channel_id=1, source_target_pairs={{0,1},{1,0},{2,3},{3,2},{4,5},{5,4},{6,7},{7,6},{8,9},{9,8},{10,11... | collective-permute-start | bytes 786440 | tf_op jit(solution)/shard_map/ppermute | solution.py:40
  122.8 3.0 %collective-permute-start.35 = (f32[2,256,128]{2,1,0:T(8,128)S(1)}, f32[2,256,128]{2,1,0:T(8,128)S(1)}, u32[]{:S(2)}, u32[]{:S(2)}) collective-permute-start(f32[2,256,128]{2,1,0:T(8,128)S(1)} %stack.22.near), channel_id=1, source_target_pairs={{0,1},{1,0},{2,3},{3,2},{4,5},{5,4},{6,7},{7,6},{8,9},{9,8},{10,11... | collective-permute-start | bytes 786440 | tf_op jit(solution)/shard_map/ppermute | solution.py:40
  126.6 10.7 %collective-permute-start.38 = (f32[512,128]{1,0:T(8,128)S(1)}, f32[512,128]{1,0:T(8,128)S(1)}, u32[]{:S(2)}, u32[]{:S(2)}) collective-permute-start(f32[512,128]{1,0:T(8,128)S(1)} %predict.11), channel_id=1, source_target_pairs={{0,128},{16,144},{32,160},{48,176},{64,192},{80,208},{96,224},{112... | collective-permute-start | bytes 786440 | tf_op jit(solution)/shard_map/ppermute | solution.py:40
  127.5 15.0 %collective-permute-start.40 = (f32[512,128]{1,0:T(8,128)S(1)}, f32[512,128]{1,0:T(8,128)S(1)}, u32[]{:S(2)}, u32[]{:S(2)}) collective-permute-start(f32[512,128]{1,0:T(8,128)S(1)} %predict.13), channel_id=1, source_target_pairs={{0,192},{16,208},{32,224},{48,240},{64,128},{80,144},{96,160},{112... | collective-permute-start | bytes 786440 | tf_op jit(solution)/shard_map/ppermute | solution.py:40
  130.2 12.3 %collective-permute-start.39 = (f32[512,128]{1,0:T(8,128)S(1)}, f32[512,128]{1,0:T(8,128)S(1)}, u32[]{:S(2)}, u32[]{:S(2)}) collective-permute-start(f32[512,128]{1,0:T(8,128)S(1)} %predict.12), channel_id=1, source_target_pairs={{0,64},{16,80},{32,96},{48,112},{64,0},{80,16},{96,32},{112,48},{1... | collective-permute-start | bytes 786440 | tf_op jit(solution)/shard_map/ppermute | solution.py:40
  142.5 4.9 %collective-permute-start.41 = (f32[128,128]{1,0:T(8,128)S(1)}, f32[128,128]{1,0:T(8,128)S(1)}, u32[]{:S(2)}, u32[]{:S(2)}) collective-permute-start(f32[128,128]{1,0:T(8,128)S(1)} %get-tuple-element.79), channel_id=1, source_target_pairs={{0,16},{16,0},{32,48},{48,32},{64,80},{80,64},{96,112},{112,96},{1... | collective-permute-start | bytes 196616 | tf_op jit(solution)/shard_map/ppermute | solution.py:40
  143.2 6.5 %collective-permute-start.42 = (f32[128,128]{1,0:T(8,128)S(1)}, f32[128,128]{1,0:T(8,128)S(1)}, u32[]{:S(2)}, u32[]{:S(2)}) collective-permute-start(f32[128,128]{1,0:T(8,128)S(1)} %get-tuple-element.80), channel_id=1, source_target_pairs={{0,32},{16,48},{32,0},{48,16},{64,96},{80,112},{96,64},{112,80},{1... | collective-permute-start | bytes 196616 | tf_op jit(solution)/shard_map/ppermute | solution.py:40
  145.1 7.0 %collective-permute-start.43 = (f32[128,128]{1,0:T(8,128)S(1)}, f32[128,128]{1,0:T(8,128)S(1)}, u32[]{:S(2)}, u32[]{:S(2)}) collective-permute-start(f32[128,128]{1,0:T(8,128)S(1)} %get-tuple-element.81), channel_id=1, source_target_pairs={{0,48},{16,32},{32,16},{48,0},{64,112},{80,96},{96,80},{112,64},{1... | collective-permute-start | bytes 196616 | tf_op jit(solution)/shard_map/ppermute | solution.py:40
  (1 other events, 1.8 us)

commit v2 on v1

--- a/solution.py
+++ b/solution.py
@@ -513,11 +513,13 @@
     odd = expand(1, 0, where, high, low, wide, [sums[0]])
     even = expand(0, 0, where, high, low, wide, [sums[0]])
     later = sum_pairs(even, swap(odd, "narrow", 1))
-    total = [sums[0]] + [swap(sums[d], "narrow", 2 * d) for d in (1, 2, 3)]
+    total = sum_two(sums[0], swap(sums[2], "narrow", 4))
+    total = [total] + [swap(sums[d], "narrow", 2 * d) for d in (1, 3)]
     total = sum_blocks(total, [later[0]])[0]
     mirror = swap(total, "narrow", 8)
     crosses += cross_halves(hot, lengths, sources[2:5], [total])
-    total = [later[0]] + [swap(later[d], "narrow", 2 * d) for d in (1, 2, 3)]
+    total = sum_two(later[0], swap(later[2], "narrow", 4))
+    total = [total] + [swap(later[d], "narrow", 2 * d) for d in (1, 3)]
     block, coefficients = sum_blocks(total + [mirror], [crosses[4][0]], 2)
 
     mirror = swap(block, "narrow", 8)

time: 153 us -> 151 us (0.987)
  starting transfers between devices: 62.5 us -> 58.3 us
  waiting for transfers between devices: 46.5 us -> 48.1 us
    ppermute x44, starting transfers between devices: 62.5 us -> 58.3 us  [swap(): return lax.ppermute(value, axis, [(i, i ^ bits) for i in range(16)])]
    ppermute x44, waiting for transfers between devices: 46.5 us -> 48.1 us  [swap(): return lax.ppermute(value, axis, [(i, i ^ bits) for i in range(16)])]
where the time goes in v2:
time: 151 us
  starting transfers between devices  58.3 us (39%)
  waiting for transfers between devices  48.1 us (32%)
  Pallas kernels  41.5 us (27%)
  between operations  2.42 us (2%)
    ppermute x44, starting transfers between devices, swap(): return lax.ppermute(value, axis, [(i, i ^ bits) for i in range(16)])  58.3 us
    ppermute x44, waiting for transfers between devices, swap(): return lax.ppermute(value, axis, [(i, i ^ bits) for i in range(16)])  48.1 us
    pallas_call x3, Pallas kernels, cross_halves(): pl.pallas_call(functools.partial(cross_kernel, firsts), in_specs=here(2 +...  11.7 us
    pallas_call x7, Pallas kernels, predict(): pl.pallas_call(functools.partial(predict_kernel, first, near_first, total...  11.6 us
    pallas_call x4, Pallas kernels, expand(): pl.pallas_call(functools.partial(expand_kernel, core, far), in_specs=scal...  5.58 us
    pallas_call x1, Pallas kernels, halves(): pl.pallas_call(halves_kernel, in_specs=anywhere(1), out_specs=here(2), ou...  3.61 us
  transfers between devices with their start and end apart: 44, of which 21 were waited for; matrix products, arithmetic and copies ran while one was open for 0% of the time, Pallas kernels for 21%

profile of v2, /device:TPU:32, one launch (start us, length us, event | category | flops | bytes accessed | tf_op | source)
XLA Modules:
  0.0 150.5 jit_solution(1376566408298573857)
XLA Ops:
  1.7 6.4 %collective-permute-start.3 = (f32[136,256]{1,0:T(8,128)S(1)}, f32[136,256]{1,0:T(8,128)S(1)}, u32[]{:S(2)}, u32[]{:S(2)}) collective-permute-start(f32[136,256]{1,0:T(8,128)S(1)} %own_observations.1.refs_0_), channel_id=1, source_target_pairs={{0,8},{1,9},{2,10},{3,11},{4,12},{5,13},{6,14},{7,15},{8,0},{9,1},... | collective-permute-start | bytes 417800 | tf_op jit(solution)/shard_map/ppermute | solution.py:40
  8.1 1.6 %collective-permute-start = (f32[136,256]{1,0:T(8,128)S(1)}, f32[136,256]{1,0:T(8,128)S(1)}, u32[]{:S(2)}, u32[]{:S(2)}) collective-permute-start(f32[136,256]{1,0:T(8,128)S(1)} %own_observations.1.refs_0_), channel_id=1, source_target_pairs={{0,2},{1,3},{2,0},{3,1},{4,6},{5,7},{6,4},{7,5},{8,10},{9,11},{10,... | collective-permute-start | bytes 417800 | tf_op jit(solution)/shard_map/ppermute | solution.py:40
  9.7 2.9 %collective-permute-start.1 = (f32[136,256]{1,0:T(8,128)S(1)}, f32[136,256]{1,0:T(8,128)S(1)}, u32[]{:S(2)}, u32[]{:S(2)}) collective-permute-start(f32[136,256]{1,0:T(8,128)S(1)} %own_observations.1.refs_0_), channel_id=1, source_target_pairs={{0,4},{1,5},{2,6},{3,7},{4,0},{5,1},{6,2},{7,3},{8,12},{9,13},{10,... | collective-permute-start | bytes 417800 | tf_op jit(solution)/shard_map/ppermute | solution.py:40
  12.8 3.6 %basis_halves.1 = (bf16[4096,512]{1,0:T(8,128)(2,1)S(1)}, bf16[4096,512]{1,0:T(8,128)(2,1)S(1)}) custom-call(f32[4096,512]{1,0:T(8,128)} %basis.1), custom_call_target="tpu_custom_call" | custom-call | flops 1 | bytes 1 | tf_op jit(solution)/shard_map/basis_halves/pallas_call | solution.py:91
  16.4 2.3 %collective-permute-done.1.refs_2_ = f32[136,256]{1,0:T(8,128)S(1)} collective-permute-done((f32[136,256]{1,0:T(8,128)S(1)}, f32[136,256]{1,0:T(8,128)S(1)}, u32[]{:S(2)}, u32[]{:S(2)}) %collective-permute-start.1) | collective-permute-done | bytes 139296 | tf_op jit(solution)/shard_map/ppermute | solution.py:40
  18.8 2.0 %collective-permute-done.2.refs_3_ = f32[136,256]{1,0:T(8,128)S(1)} collective-permute-done((f32[136,256]{1,0:T(8,128)S(1)}, f32[136,256]{1,0:T(8,128)S(1)}, u32[]{:S(2)}, u32[]{:S(2)}) %collective-permute-start.2) | collective-permute-done | bytes 139296 | tf_op jit(solution)/shard_map/ppermute | solution.py:40
  21.0 2.2 %collective-permute-start.8 = (f32[136,256]{1,0:T(8,128)S(1)}, f32[136,256]{1,0:T(8,128)S(1)}, u32[]{:S(2)}, u32[]{:S(2)}) collective-permute-start(f32[136,256]{1,0:T(8,128)S(1)} %collective-permute-done.3.refs_5_.refs_0_), channel_id=1, source_target_pairs={{0,6},{1,7},{2,4},{3,5},{4,2},{5,3},{6,0},{7,1},{8,14},{9,15},{10,... | collective-permute-start | bytes 417800 | tf_op jit(solution)/shard_map/ppermute | solution.py:40
  23.2 1.3 collective-permute-start.5
  24.5 4.5 %collective-permute-done.7.refs_0_ = f32[136,256]{1,0:T(8,128)S(1)} collective-permute-done((f32[136,256]{1,0:T(8,128)S(1)}, f32[136,256]{1,0:T(8,128)S(1)}, u32[]{:S(2)}, u32[]{:S(2)}) %collective-permute-start.7) | collective-permute-done | bytes 139296 | tf_op jit(solution)/shard_map/ppermute | solution.py:40
  29.0 2.2 %collective-permute-done.8.refs_1_ = f32[136,256]{1,0:T(8,128)S(1)} collective-permute-done((f32[136,256]{1,0:T(8,128)S(1)}, f32[136,256]{1,0:T(8,128)S(1)}, u32[]{:S(2)}, u32[]{:S(2)}) %collective-permute-start.8) | collective-permute-done | bytes 139296 | tf_op jit(solution)/shard_map/ppermute | solution.py:40
  31.9 1.7 %project_near.1.before = f32[128,512]{1,0:T(8,128)S(1)} custom-call(s32[2]{0:T(128)S(1)} %pad_add_fusion.where, bf16[4096,512]{1,0:T(8,128)(2,1)S(1)} %get-tuple-element.42.refs_4_.high, bf16[4096,512]{1,0:T(8,128)(2,1)S(1)} %get-tuple-element.43.low, f32[4,136,256]{2,1,0:T(8,128)S(1)} %stack.18.near.refs_0_, ...), custom_call_target="tpu_custom_call" | custom-call | flops 1 | bytes 1 | tf_op jit(solution)/shard_map/project_near/pallas_call | solution.py:155
  33.7 1.8 %project.1 = (f32[40,512]{1,0:T(8,128)S(1)}, f32[40,512]{1,0:T(8,128)S(1)}, f32[40,512]{1,0:T(8,128)S(1)}, f32[40,512]{1,0:T(8,128)S(1)}) custom-call(s32[2]{0:T(128)S(1)} %pad_add_fusion.where, bf16[4096,512]{1,0:T(8,128)(2,1)S(1)} %get-tuple-element.42.refs_4_.high, bf16[4096,512]{1,0:T(8,128)(2,1)S(1)} %get-tuple-element.43.low, f32[128,128]{1,0:T(8,128)S(1)} %copy-done, ...), custom_call_target="tpu_custom_call" | custom-call | flops 1 | bytes 1 | tf_op jit(solution)/shard_map/project/pallas_call | solution.py:180
  35.5 1.6 %collective-permute-start.10 = (f32[40,512]{1,0:T(8,128)S(1)}, f32[40,512]{1,0:T(8,128)S(1)}, u32[]{:S(2)}, u32[]{:S(2)}) collective-permute-start(f32[40,512]{1,0:T(8,128)S(1)} %get-tuple-element.45), channel_id=1, source_target_pairs={{0,64},{16,80},{32,96},{48,112},{64,0},{80,16},{96,32},{112,48},{1... | collective-permute-start | bytes 245768 | tf_op jit(solution)/shard_map/ppermute | solution.py:40
  37.1 2.7 %collective-permute-start.11 = (f32[40,512]{1,0:T(8,128)S(1)}, f32[40,512]{1,0:T(8,128)S(1)}, u32[]{:S(2)}, u32[]{:S(2)}) collective-permute-start(f32[40,512]{1,0:T(8,128)S(1)} %get-tuple-element.46), channel_id=1, source_target_pairs={{0,128},{16,144},{32,160},{48,176},{64,192},{80,208},{96,224},{112... | collective-permute-start | bytes 245768 | tf_op jit(solution)/shard_map/ppermute | solution.py:40
  40.3 3.7 %collective-permute-done.11.b = f32[40,512]{1,0:T(8,128)S(1)} collective-permute-done((f32[40,512]{1,0:T(8,128)S(1)}, f32[40,512]{1,0:T(8,128)S(1)}, u32[]{:S(2)}, u32[]{:S(2)}) %collective-permute-start.11) | collective-permute-done | bytes 81952 | tf_op jit(solution)/shard_map/ppermute | solution.py:40
  44.0 1.7 %collective-permute-done.12.c = f32[40,512]{1,0:T(8,128)S(1)} collective-permute-done((f32[40,512]{1,0:T(8,128)S(1)}, f32[40,512]{1,0:T(8,128)S(1)}, u32[]{:S(2)}, u32[]{:S(2)}) %collective-permute-start.12) | collective-permute-done | bytes 81952 | tf_op jit(solution)/shard_map/ppermute | solution.py:40
  46.8 1.5 collective-permute-start.14
  50.8 2.8 %collective-permute-done.14.b = f32[40,512]{1,0:T(8,128)S(1)} collective-permute-done((f32[40,512]{1,0:T(8,128)S(1)}, f32[40,512]{1,0:T(8,128)S(1)}, u32[]{:S(2)}, u32[]{:S(2)}) %collective-permute-start.14) | collective-permute-done | bytes 81952 | tf_op jit(solution)/shard_map/ppermute | solution.py:40
  53.7 2.3 %collective-permute-done.15.c = f32[40,512]{1,0:T(8,128)S(1)} collective-permute-done((f32[40,512]{1,0:T(8,128)S(1)}, f32[40,512]{1,0:T(8,128)S(1)}, u32[]{:S(2)}, u32[]{:S(2)}) %collective-permute-start.15) | collective-permute-done | bytes 81952 | tf_op jit(solution)/shard_map/ppermute | solution.py:40
  56.9 2.6 %collective-permute-start.17 = (f32[32,512]{1,0:T(8,128)S(1)}, f32[32,512]{1,0:T(8,128)S(1)}, u32[]{:S(2)}, u32[]{:S(2)}) collective-permute-start(f32[32,512]{1,0:T(8,128)S(1)} %get-tuple-element.48.a), channel_id=1, source_target_pairs={{0,128},{16,144},{32,160},{48,176},{64,192},{80,208},{96,224},{112... | collective-permute-start | bytes 196616 | tf_op jit(solution)/shard_map/ppermute | solution.py:40
  59.4 2.1 %collective-permute-start.18 = (f32[32,512]{1,0:T(8,128)S(1)}, f32[32,512]{1,0:T(8,128)S(1)}, u32[]{:S(2)}, u32[]{:S(2)}) collective-permute-start(f32[32,512]{1,0:T(8,128)S(1)} %get-tuple-element.48.a), channel_id=1, source_target_pairs={{0,192},{16,208},{32,224},{48,240},{64,128},{80,144},{96,160},{112... | collective-permute-start | bytes 196616 | tf_op jit(solution)/shard_map/ppermute | solution.py:40
  62.3 2.9 %cross.3 = (bf16[2048,512]{1,0:T(8,128)(2,1)S(1)}, bf16[2048,512]{1,0:T(8,128)(2,1)S(1)}, bf16[2048,512]{1,0:T(8,128)(2,1)S(1)}, bf16[2048,512]{1,0:T(8,128)(2,1)S(1)}) custom-call(bf16[2048,128]{1,0:T(8,128)(2,1)S(1)} %get-tuple-element.50.hot, f32[128,128]{1,0:T(8,128)S(1)} %get-tuple-element.51.lengths, f32[4,136,256]{2,1,0:T(8,128)S(1)} %stack.18.near.refs_0_, ...), custom_call_target="tpu_custom_call" | custom-call | flops 1 | bytes 1 | tf_op jit(solution)/shard_map/cross/pallas_call | solution.py:377
  66.2 1.4 expand.5
  67.7 1.4 expand.4.mine
  69.7 1.4 expand.7
  73.1 2.3 %collective-permute-start.26 = (f32[256,128]{1,0:T(8,128)S(1)}, f32[256,128]{1,0:T(8,128)S(1)}, u32[]{:S(2)}, u32[]{:S(2)}) collective-permute-start(f32[256,128]{1,0:T(8,128)S(1)} %get-tuple-element.60), channel_id=1, source_target_pairs={{0,6},{1,7},{2,4},{3,5},{4,2},{5,3},{6,0},{7,1},{8,14},{9,15},{10,... | collective-permute-start | bytes 393224 | tf_op jit(solution)/shard_map/ppermute | solution.py:40
  75.4 1.4 expand.6.mine
  76.8 2.3 %collective-permute-done.24.b = f32[256,128]{1,0:T(8,128)S(1)} collective-permute-done((f32[256,128]{1,0:T(8,128)S(1)}, f32[256,128]{1,0:T(8,128)S(1)}, u32[]{:S(2)}, u32[]{:S(2)}) %collective-permute-start.24) | collective-permute-done | bytes 131104 | tf_op jit(solution)/shard_map/ppermute | solution.py:40
  79.7 1.7 %collective-permute-done.26.refs_2_ = f32[256,128]{1,0:T(8,128)S(1)} collective-permute-done((f32[256,128]{1,0:T(8,128)S(1)}, f32[256,128]{1,0:T(8,128)S(1)}, u32[]{:S(2)}, u32[]{:S(2)}) %collective-permute-start.26) | collective-permute-done | bytes 131104 | tf_op jit(solution)/shard_map/ppermute | solution.py:40
  82.4 1.8 %collective-permute-start.21 = (f32[256,128]{1,0:T(8,128)S(1)}, f32[256,128]{1,0:T(8,128)S(1)}, u32[]{:S(2)}, u32[]{:S(2)}) collective-permute-start(f32[256,128]{1,0:T(8,128)S(1)} %get-tuple-element.55), channel_id=1, source_target_pairs={{0,4},{1,5},{2,6},{3,7},{4,0},{5,1},{6,2},{7,3},{8,12},{9,13},{10,... | collective-permute-start | bytes 393224 | tf_op jit(solution)/shard_map/ppermute | solution.py:40
  86.4 4.4 %cross.4 = (bf16[2048,512]{1,0:T(8,128)(2,1)S(1)}, bf16[2048,512]{1,0:T(8,128)(2,1)S(1)}, bf16[2048,512]{1,0:T(8,128)(2,1)S(1)}, bf16[2048,512]{1,0:T(8,128)(2,1...) custom-call(bf16[2048,128]{1,0:T(8,128)(2,1)S(1)} %get-tuple-element.50.hot, ...), custom_call_target="tpu_custom_call" | custom-call | flops 1 | bytes 1 | tf_op jit(solution)/shard_map/cross/pallas_call | solution.py:377
  90.9 2.8 %collective-permute-done.27.refs_3_ = f32[256,128]{1,0:T(8,128)S(1)} collective-permute-done((f32[256,128]{1,0:T(8,128)S(1)}, f32[256,128]{1,0:T(8,128)S(1)}, u32[]{:S(2)}, u32[]{:S(2)}) %collective-permute-start.27) | collective-permute-done | bytes 131104 | tf_op jit(solution)/shard_map/ppermute | solution.py:40
  94.3 3.2 %collective-permute-start.28 = (f32[256,128]{1,0:T(8,128)S(1)}, f32[256,128]{1,0:T(8,128)S(1)}, u32[]{:S(2)}, u32[]{:S(2)}) collective-permute-start(f32[256,128]{1,0:T(8,128)S(1)} %get-tuple-element.63.refs_3_.refs_0_), channel_id=1, source_target_pairs={{0,8},{1,9},{2,10},{3,11},{4,12},{5,13},{6,14},{7,15},{8,0},{9,1},... | collective-permute-start | bytes 393224 | tf_op jit(solution)/shard_map/ppermute | solution.py:40
  97.6 2.8 %collective-permute-start.32 = (f32[256,128]{1,0:T(8,128)S(1)}, f32[256,128]{1,0:T(8,128)S(1)}, u32[]{:S(2)}, u32[]{:S(2)}) collective-permute-start(f32[256,128]{1,0:T(8,128)S(1)} %get-tuple-element.63.refs_3_.refs_0_), channel_id=1, source_target_pairs={{0,4},{1,5},{2,6},{3,7},{4,0},{5,1},{6,2},{7,3},{8,12},{9,13},{10,... | collective-permute-start | bytes 393224 | tf_op jit(solution)/shard_map/ppermute | solution.py:40
  100.4 1.9 %collective-permute-start.33 = (f32[256,128]{1,0:T(8,128)S(1)}, f32[256,128]{1,0:T(8,128)S(1)}, u32[]{:S(2)}, u32[]{:S(2)}) collective-permute-start(f32[256,128]{1,0:T(8,128)S(1)} %get-tuple-element.63.refs_3_.refs_0_), channel_id=1, source_target_pairs={{0,6},{1,7},{2,4},{3,5},{4,2},{5,3},{6,0},{7,1},{8,14},{9,15},{10,... | collective-permute-start | bytes 393224 | tf_op jit(solution)/shard_map/ppermute | solution.py:40
  102.3 4.4 %cross.5 = (bf16[2048,512]{1,0:T(8,128)(2,1)S(1)}, bf16[2048,512]{1,0:T(8,128)(2,1)S(1)}, bf16[2048,512]{1,0:T(8,128)(2,1)S(1)}, bf16[2048,512]{1,0:T(8,128)(2,1...) custom-call(bf16[2048,128]{1,0:T(8,128)(2,1)S(1)} %get-tuple-element.50.hot, ...), custom_call_target="tpu_custom_call" | custom-call | flops 1 | bytes 1 | tf_op jit(solution)/shard_map/cross/pallas_call | solution.py:377
  107.4 3.7 %collective-permute-start.29 = (f32[256,128]{1,0:T(8,128)S(1)}, f32[256,128]{1,0:T(8,128)S(1)}, u32[]{:S(2)}, u32[]{:S(2)}) collective-permute-start(f32[256,128]{1,0:T(8,128)S(1)} %collective-permute-done.28.refs_4_.refs_0_), channel_id=1, source_target_pairs={{0,4},{1,5},{2,6},{3,7},{4,0},{5,1},{6,2},{7,3},{8,12},{9,13},{10,... | collective-permute-start | bytes 393224 | tf_op jit(solution)/shard_map/ppermute | solution.py:40
  112.1 2.9 %predict.7.refs_0_.refs_2_ = f32[2048,128]{1,0:T(8,128)S(1)} custom-call(f32[4,256,128]{2,1,0:T(8,128)S(1)} %stack.21.near, f32[4,256,128]{2,1,0:T(8,128)S(1)} %collective-permute-done.34.other, bf16[2048,512]{1,0:T(8,128)(2,1)S(1)} %get-tuple-element.52.refs_0_.h0, bf16[2048,512]{1,0:T(8,128)(2,1)S(1)} %get-tuple-element.69.l0, ...), custom_call_target="tpu_custom_call" | custom-call | flops 1 | bytes 1 | tf_op jit(solution)/shard_map/predict/pallas_call | solution.py:414
  115.1 2.9 %predict.8.refs_2_.refs_0_ = f32[2048,128]{1,0:T(8,128)S(1)} custom-call(f32[4,256,128]{2,1,0:T(8,128)S(1)} %stack.21.near, f32[4,256,128]{2,1,0:T(8,128)S(1)} %collective-permute-done.34.other, bf16[2048,512]{1,0:T(8,128)(2,1)S(1)} %get-tuple-element.65.h0, bf16[2048,512]{1,0:T(8,128)(2,1)S(1)} %get-tuple-element.66.l0, ...), custom_call_target="tpu_custom_call" | custom-call | flops 1 | bytes 1 | tf_op jit(solution)/shard_map/predict/pallas_call | solution.py:414
  118.0 2.2 %collective-permute-done.30.refs_1_ = f32[256,128]{1,0:T(8,128)S(1)} collective-permute-done((f32[256,128]{1,0:T(8,128)S(1)}, f32[256,128]{1,0:T(8,128)S(1)}, u32[]{:S(2)}, u32[]{:S(2)}) %collective-permute-start.30) | collective-permute-done | bytes 131104 | tf_op jit(solution)/shard_map/ppermute | solution.py:40
  120.4 2.9 %predict.9.refs_0_ = f32[2048,128]{1,0:T(8,128)S(1)} custom-call(f32[2,256,128]{2,1,0:T(8,128)S(1)} %stack.23.near, f32[2,256,128]{2,1,0:T(8,128)S(1)} %collective-permute-done.37.other, bf16[2048,512]{1,0:T(8,128)(2,1)S(1)} %get-tuple-element.61.refs_4_.h0, bf16[2048,512]{1,0:T(8,128)(2,1)S(1)} %get-tuple-element.75.l0, ...), custom_call_target="tpu_custom_call" | custom-call | flops 1 | bytes 1 | tf_op jit(solution)/shard_map/predict/pallas_call | solution.py:414
  125.0 2.0 %collective-permute-start.40 = (f32[512,128]{1,0:T(8,128)S(1)}, f32[512,128]{1,0:T(8,128)S(1)}, u32[]{:S(2)}, u32[]{:S(2)}) collective-permute-start(f32[512,128]{1,0:T(8,128)S(1)} %predict.13), channel_id=1, source_target_pairs={{0,192},{16,208},{32,224},{48,240},{64,128},{80,144},{96,160},{112... | collective-permute-start | bytes 786440 | tf_op jit(solution)/shard_map/ppermute | solution.py:40
  127.6 1.6 %collective-permute-start.39 = (f32[512,128]{1,0:T(8,128)S(1)}, f32[512,128]{1,0:T(8,128)S(1)}, u32[]{:S(2)}, u32[]{:S(2)}) collective-permute-start(f32[512,128]{1,0:T(8,128)S(1)} %predict.12), channel_id=1, source_target_pairs={{0,64},{16,80},{32,96},{48,112},{64,0},{80,16},{96,32},{112,48},{1... | collective-permute-start | bytes 786440 | tf_op jit(solution)/shard_map/ppermute | solution.py:40
  129.9 4.8 %collective-permute-done.38.b = f32[512,128]{1,0:T(8,128)S(1)} collective-permute-done((f32[512,128]{1,0:T(8,128)S(1)}, f32[512,128]{1,0:T(8,128)S(1)}, u32[]{:S(2)}, u32[]{:S(2)}) %collective-permute-start.38) | collective-permute-done | bytes 262176 | tf_op jit(solution)/shard_map/ppermute | solution.py:40
  134.8 5.1 %collective-permute-done.40.c = f32[512,128]{1,0:T(8,128)S(1)} collective-permute-done((f32[512,128]{1,0:T(8,128)S(1)}, f32[512,128]{1,0:T(8,128)S(1)}, u32[]{:S(2)}, u32[]{:S(2)}) %collective-permute-start.40) | collective-permute-done | bytes 262176 | tf_op jit(solution)/shard_map/ppermute | solution.py:40
  140.7 1.9 %collective-permute-start.42 = (f32[128,128]{1,0:T(8,128)S(1)}, f32[128,128]{1,0:T(8,128)S(1)}, u32[]{:S(2)}, u32[]{:S(2)}) collective-permute-start(f32[128,128]{1,0:T(8,128)S(1)} %get-tuple-element.80), channel_id=1, source_target_pairs={{0,32},{16,48},{32,0},{48,16},{64,96},{80,112},{96,64},{112,80},{1... | collective-permute-start | bytes 196616 | tf_op jit(solution)/shard_map/ppermute | solution.py:40
  144.9 2.3 %collective-permute-done.42.c = f32[128,128]{1,0:T(8,128)S(1)} collective-permute-done((f32[128,128]{1,0:T(8,128)S(1)}, f32[128,128]{1,0:T(8,128)S(1)}, u32[]{:S(2)}, u32[]{:S(2)}) %collective-permute-start.42) | collective-permute-done | bytes 65568 | tf_op jit(solution)/shard_map/ppermute | solution.py:40
  147.2 2.3 %collective-permute-done.43.d = f32[128,128]{1,0:T(8,128)S(1)} collective-permute-done((f32[128,128]{1,0:T(8,128)S(1)}, f32[128,128]{1,0:T(8,128)S(1)}, u32[]{:S(2)}, u32[]{:S(2)}) %collective-permute-start.43) | collective-permute-done | bytes 65568 | tf_op jit(solution)/shard_map/ppermute | solution.py:40
  (88 shorter events, 23.9 us)
Async XLA Ops:
  1.7 14.7 %collective-permute-start.3 = (f32[136,256]{1,0:T(8,128)S(1)}, f32[136,256]{1,0:T(8,128)S(1)}, u32[]{:S(2)}, u32[]{:S(2)}) collective-permute-start(f32[136,256]{1,0:T(8,128)S(1)} %own_observations.1.refs_0_), channel_id=1, source_target_pairs={{0,8},{1,9},{2,10},{3,11},{4,12},{5,13},{6,14},{7,15},{8,0},{9,1},... | collective-permute-start | bytes 417800 | tf_op jit(solution)/shard_map/ppermute | solution.py:40
  8.1 8.3 %collective-permute-start = (f32[136,256]{1,0:T(8,128)S(1)}, f32[136,256]{1,0:T(8,128)S(1)}, u32[]{:S(2)}, u32[]{:S(2)}) collective-permute-start(f32[136,256]{1,0:T(8,128)S(1)} %own_observations.1.refs_0_), channel_id=1, source_target_pairs={{0,2},{1,3},{2,0},{3,1},{4,6},{5,7},{6,4},{7,5},{8,10},{9,11},{10,... | collective-permute-start | bytes 417800 | tf_op jit(solution)/shard_map/ppermute | solution.py:40
  9.7 9.1 %collective-permute-start.1 = (f32[136,256]{1,0:T(8,128)S(1)}, f32[136,256]{1,0:T(8,128)S(1)}, u32[]{:S(2)}, u32[]{:S(2)}) collective-permute-start(f32[136,256]{1,0:T(8,128)S(1)} %own_observations.1.refs_0_), channel_id=1, source_target_pairs={{0,4},{1,5},{2,6},{3,7},{4,0},{5,1},{6,2},{7,3},{8,12},{9,13},{10,... | collective-permute-start | bytes 417800 | tf_op jit(solution)/shard_map/ppermute | solution.py:40
  12.6 8.2 %collective-permute-start.2 = (f32[136,256]{1,0:T(8,128)S(1)}, f32[136,256]{1,0:T(8,128)S(1)}, u32[]{:S(2)}, u32[]{:S(2)}) collective-permute-start(f32[136,256]{1,0:T(8,128)S(1)} %own_observations.1.refs_0_), channel_id=1, source_target_pairs={{0,6},{1,7},{2,4},{3,5},{4,2},{5,3},{6,0},{7,1},{8,14},{9,15},{10,... | collective-permute-start | bytes 417800 | tf_op jit(solution)/shard_map/ppermute | solution.py:40
  20.8 11.1 %collective-permute-start.4 = (f32[4,136,256]{2,1,0:T(8,128)S(1)}, f32[4,136,256]{2,1,0:T(8,128)S(1)}, u32[]{:S(2)}, u32[]{:S(2)}) collective-permute-start(f32[4,136,256]{2,1,0:T(8,128)S(1)} %stack.18.near.refs_0_), channel_id=1, source_target_pairs={{0,1},{1,0},{2,3},{3,2},{4,5},{5,4},{6,7},{7,6},{8,9},{9,8},{10,11... | collective-permute-start | bytes 1671176 | tf_op jit(solution)/shard_map/ppermute | solution.py:40
  20.9 8.1 %collective-permute-start.7 = (f32[136,256]{1,0:T(8,128)S(1)}, f32[136,256]{1,0:T(8,128)S(1)}, u32[]{:S(2)}, u32[]{:S(2)}) collective-permute-start(f32[136,256]{1,0:T(8,128)S(1)} %collective-permute-done.3.refs_5_.refs_0_), channel_id=1, source_target_pairs={{0,4},{1,5},{2,6},{3,7},{4,0},{5,1},{6,2},{7,3},{8,12},{9,13},{10,... | collective-permute-start | bytes 417800 | tf_op jit(solution)/shard_map/ppermute | solution.py:40
  21.0 10.2 %collective-permute-start.8 = (f32[136,256]{1,0:T(8,128)S(1)}, f32[136,256]{1,0:T(8,128)S(1)}, u32[]{:S(2)}, u32[]{:S(2)}) collective-permute-start(f32[136,256]{1,0:T(8,128)S(1)} %collective-permute-done.3.refs_5_.refs_0_), channel_id=1, source_target_pairs={{0,6},{1,7},{2,4},{3,5},{4,2},{5,3},{6,0},{7,1},{8,14},{9,15},{10,... | collective-permute-start | bytes 417800 | tf_op jit(solution)/shard_map/ppermute | solution.py:40
  23.2 8.1 %collective-permute-start.5 = (f32[136,256]{1,0:T(8,128)S(1)}, f32[136,256]{1,0:T(8,128)S(1)}, u32[]{:S(2)}, u32[]{:S(2)}) collective-permute-start(f32[136,256]{1,0:T(8,128)S(1)} %collective-permute-done.3.refs_5_.refs_0_), channel_id=1, source_target_pairs={{0,2},{1,3},{2,0},{3,1},{4,6},{5,7},{6,4},{7,5},{8,10},{9,11},{10,... | collective-permute-start | bytes 417800 | tf_op jit(solution)/shard_map/ppermute | solution.py:40
  31.2 2.5 %collective-permute-start.9 = (f32[2,136,256]{2,1,0:T(8,128)S(1)}, f32[2,136,256]{2,1,0:T(8,128)S(1)}, u32[]{:S(2)}, u32[]{:S(2)}) collective-permute-start(f32[2,136,256]{2,1,0:T(8,128)S(1)} %stack.20.near1.refs_1_), channel_id=1, source_target_pairs={{0,1},{1,0},{2,3},{3,2},{4,5},{5,4},{6,7},{7,6},{8,9},{9,8},{10,11... | collective-permute-start | bytes 835592 | tf_op jit(solution)/shard_map/ppermute | solution.py:40
  31.3 2.3 %collective-permute-start.6 = (f32[2,136,256]{2,1,0:T(8,128)S(1)}, f32[2,136,256]{2,1,0:T(8,128)S(1)}, u32[]{:S(2)}, u32[]{:S(2)}) collective-permute-start(f32[2,136,256]{2,1,0:T(8,128)S(1)} %stack.19.near0.refs_2_), channel_id=1, source_target_pairs={{0,1},{1,0},{2,3},{3,2},{4,5},{5,4},{6,7},{7,6},{8,9},{9,8},{10,11... | collective-permute-start | bytes 835592 | tf_op jit(solution)/shard_map/ppermute | solution.py:40
  31.9 1.8 %copy-start.1 = (s32[2048]{0:T(1024)S(1)}, s32[2048]{0:T(1024)}, u32[]{:S(2)}) copy-start(s32[2048]{0:T(1024)} %param.19) | copy-start | bytes 24580
  33.7 22.3 %copy-start.2 = (f32[512]{0:T(512)S(1)}, f32[512]{0:T(512)}, u32[]{:S(2)}) copy-start(f32[512]{0:T(512)} %param.11) | copy-start | bytes 6148
  33.7 22.3 %copy-start.3 = (f32[128]{0:T(128)S(1)}, f32[128]{0:T(128)}, u32[]{:S(2)}) copy-start(f32[128]{0:T(128)} %param.13) | copy-start | bytes 1540
  33.7 27.8 %copy-start.4 = (f32[10]{0:T(128)S(1)}, f32[10]{0:T(128)}, u32[]{:S(2)}) copy-start(f32[10]{0:T(128)} %length_scales.1) | copy-start | bytes 124
  35.5 4.8 %collective-permute-start.10 = (f32[40,512]{1,0:T(8,128)S(1)}, f32[40,512]{1,0:T(8,128)S(1)}, u32[]{:S(2)}, u32[]{:S(2)}) collective-permute-start(f32[40,512]{1,0:T(8,128)S(1)} %get-tuple-element.45), channel_id=1, source_target_pairs={{0,64},{16,80},{32,96},{48,112},{64,0},{80,16},{96,32},{112,48},{1... | collective-permute-start | bytes 245768 | tf_op jit(solution)/shard_map/ppermute | solution.py:40
  37.1 6.9 %collective-permute-start.11 = (f32[40,512]{1,0:T(8,128)S(1)}, f32[40,512]{1,0:T(8,128)S(1)}, u32[]{:S(2)}, u32[]{:S(2)}) collective-permute-start(f32[40,512]{1,0:T(8,128)S(1)} %get-tuple-element.46), channel_id=1, source_target_pairs={{0,128},{16,144},{32,160},{48,176},{64,192},{80,208},{96,224},{112... | collective-permute-start | bytes 245768 | tf_op jit(solution)/shard_map/ppermute | solution.py:40
  39.8 5.9 %collective-permute-start.12 = (f32[40,512]{1,0:T(8,128)S(1)}, f32[40,512]{1,0:T(8,128)S(1)}, u32[]{:S(2)}, u32[]{:S(2)}) collective-permute-start(f32[40,512]{1,0:T(8,128)S(1)} %get-tuple-element.47), channel_id=1, source_target_pairs={{0,192},{16,208},{32,224},{48,240},{64,128},{80,144},{96,160},{112... | collective-permute-start | bytes 245768 | tf_op jit(solution)/shard_map/ppermute | solution.py:40
  45.7 5.1 %collective-permute-start.13 = (f32[40,512]{1,0:T(8,128)S(1)}, f32[40,512]{1,0:T(8,128)S(1)}, u32[]{:S(2)}, u32[]{:S(2)}) collective-permute-start(f32[40,512]{1,0:T(8,128)S(1)} %sum_over_x.1.own), channel_id=1, source_target_pairs={{0,16},{16,0},{32,48},{48,32},{64,80},{80,64},{96,112},{112,96},{1... | collective-permute-start | bytes 245768 | tf_op jit(solution)/shard_map/ppermute | solution.py:40
  46.8 6.8 %collective-permute-start.14 = (f32[40,512]{1,0:T(8,128)S(1)}, f32[40,512]{1,0:T(8,128)S(1)}, u32[]{:S(2)}, u32[]{:S(2)}) collective-permute-start(f32[40,512]{1,0:T(8,128)S(1)} %sum_over_x.1.own), channel_id=1, source_target_pairs={{0,32},{16,48},{32,0},{48,16},{64,96},{80,112},{96,64},{112,80},{1... | collective-permute-start | bytes 245768 | tf_op jit(solution)/shard_map/ppermute | solution.py:40
  48.3 7.7 %collective-permute-start.15 = (f32[40,512]{1,0:T(8,128)S(1)}, f32[40,512]{1,0:T(8,128)S(1)}, u32[]{:S(2)}, u32[]{:S(2)}) collective-permute-start(f32[40,512]{1,0:T(8,128)S(1)} %sum_over_x.1.own), channel_id=1, source_target_pairs={{0,48},{16,32},{32,16},{48,0},{64,112},{80,96},{96,80},{112,64},{1... | collective-permute-start | bytes 245768 | tf_op jit(solution)/shard_map/ppermute | solution.py:40
  56.8 8.5 %collective-permute-start.16 = (f32[32,512]{1,0:T(8,128)S(1)}, f32[32,512]{1,0:T(8,128)S(1)}, u32[]{:S(2)}, u32[]{:S(2)}) collective-permute-start(f32[32,512]{1,0:T(8,128)S(1)} %get-tuple-element.48.a), channel_id=1, source_target_pairs={{0,64},{16,80},{32,96},{48,112},{64,0},{80,16},{96,32},{112,48},{1... | collective-permute-start | bytes 196616 | tf_op jit(solution)/shard_map/ppermute | solution.py:40
  56.9 8.4 %collective-permute-start.17 = (f32[32,512]{1,0:T(8,128)S(1)}, f32[32,512]{1,0:T(8,128)S(1)}, u32[]{:S(2)}, u32[]{:S(2)}) collective-permute-start(f32[32,512]{1,0:T(8,128)S(1)} %get-tuple-element.48.a), channel_id=1, source_target_pairs={{0,128},{16,144},{32,160},{48,176},{64,192},{80,208},{96,224},{112... | collective-permute-start | bytes 196616 | tf_op jit(solution)/shard_map/ppermute | solution.py:40
  59.4 5.9 %collective-permute-start.18 = (f32[32,512]{1,0:T(8,128)S(1)}, f32[32,512]{1,0:T(8,128)S(1)}, u32[]{:S(2)}, u32[]{:S(2)}) collective-permute-start(f32[32,512]{1,0:T(8,128)S(1)} %get-tuple-element.48.a), channel_id=1, source_target_pairs={{0,192},{16,208},{32,224},{48,240},{64,128},{80,144},{96,160},{112... | collective-permute-start | bytes 196616 | tf_op jit(solution)/shard_map/ppermute | solution.py:40
  67.6 2.0 %collective-permute-start.19 = (f32[4,256,128]{2,1,0:T(8,128)S(1)}, f32[4,256,128]{2,1,0:T(8,128)S(1)}, u32[]{:S(2)}, u32[]{:S(2)}) collective-permute-start(f32[4,256,128]{2,1,0:T(8,128)S(1)} %expand.5), channel_id=1, source_target_pairs={{0,1},{1,0},{2,3},{3,2},{4,5},{5,4},{6,7},{7,6},{8,9},{9,8},{10,11... | collective-permute-start | bytes 1572872 | tf_op jit(solution)/shard_map/ppermute | solution.py:40
  71.1 8.1 %collective-permute-start.20 = (f32[4,256,128]{2,1,0:T(8,128)S(1)}, f32[4,256,128]{2,1,0:T(8,128)S(1)}, u32[]{:S(2)}, u32[]{:S(2)}) collective-permute-start(f32[4,256,128]{2,1,0:T(8,128)S(1)} %expand.7), channel_id=1, source_target_pairs={{0,1},{1,0},{2,3},{3,2},{4,5},{5,4},{6,7},{7,6},{8,9},{9,8},{10,11... | collective-permute-start | bytes 1572872 | tf_op jit(solution)/shard_map/ppermute | solution.py:40
  71.3 7.8 %collective-permute-start.24 = (f32[256,128]{1,0:T(8,128)S(1)}, f32[256,128]{1,0:T(8,128)S(1)}, u32[]{:S(2)}, u32[]{:S(2)}) collective-permute-start(f32[256,128]{1,0:T(8,128)S(1)} %get-tuple-element.58), channel_id=1, source_target_pairs={{0,4},{1,5},{2,6},{3,7},{4,0},{5,1},{6,2},{7,3},{8,12},{9,13},{10,... | collective-permute-start | bytes 393224 | tf_op jit(solution)/shard_map/ppermute | solution.py:40
  71.9 7.8 %collective-permute-start.25 = (f32[256,128]{1,0:T(8,128)S(1)}, f32[256,128]{1,0:T(8,128)S(1)}, u32[]{:S(2)}, u32[]{:S(2)}) collective-permute-start(f32[256,128]{1,0:T(8,128)S(1)} %get-tuple-element.59), channel_id=1, source_target_pairs={{0,2},{1,3},{2,0},{3,1},{4,6},{5,7},{6,4},{7,5},{8,10},{9,11},{10,... | collective-permute-start | bytes 393224 | tf_op jit(solution)/shard_map/ppermute | solution.py:40
  73.1 8.3 %collective-permute-start.26 = (f32[256,128]{1,0:T(8,128)S(1)}, f32[256,128]{1,0:T(8,128)S(1)}, u32[]{:S(2)}, u32[]{:S(2)}) collective-permute-start(f32[256,128]{1,0:T(8,128)S(1)} %get-tuple-element.60), channel_id=1, source_target_pairs={{0,6},{1,7},{2,4},{3,5},{4,2},{5,3},{6,0},{7,1},{8,14},{9,15},{10,... | collective-permute-start | bytes 393224 | tf_op jit(solution)/shard_map/ppermute | solution.py:40
  81.4 12.2 %collective-permute-start.27 = (f32[256,128]{1,0:T(8,128)S(1)}, f32[256,128]{1,0:T(8,128)S(1)}, u32[]{:S(2)}, u32[]{:S(2)}) collective-permute-start(f32[256,128]{1,0:T(8,128)S(1)} %sum_over_y.2.refs_3_), channel_id=1, source_target_pairs={{0,8},{1,9},{2,10},{3,11},{4,12},{5,13},{6,14},{7,15},{8,0},{9,1},... | collective-permute-start | bytes 393224 | tf_op jit(solution)/shard_map/ppermute | solution.py:40
  82.4 8.5 %collective-permute-start.21 = (f32[256,128]{1,0:T(8,128)S(1)}, f32[256,128]{1,0:T(8,128)S(1)}, u32[]{:S(2)}, u32[]{:S(2)}) collective-permute-start(f32[256,128]{1,0:T(8,128)S(1)} %get-tuple-element.55), channel_id=1, source_target_pairs={{0,4},{1,5},{2,6},{3,7},{4,0},{5,1},{6,2},{7,3},{8,12},{9,13},{10,... | collective-permute-start | bytes 393224 | tf_op jit(solution)/shard_map/ppermute | solution.py:40
  84.1 9.5 %collective-permute-start.22 = (f32[256,128]{1,0:T(8,128)S(1)}, f32[256,128]{1,0:T(8,128)S(1)}, u32[]{:S(2)}, u32[]{:S(2)}) collective-permute-start(f32[256,128]{1,0:T(8,128)S(1)} %get-tuple-element.56), channel_id=1, source_target_pairs={{0,2},{1,3},{2,0},{3,1},{4,6},{5,7},{6,4},{7,5},{8,10},{9,11},{10,... | collective-permute-start | bytes 393224 | tf_op jit(solution)/shard_map/ppermute | solution.py:40
  85.3 8.3 %collective-permute-start.23 = (f32[256,128]{1,0:T(8,128)S(1)}, f32[256,128]{1,0:T(8,128)S(1)}, u32[]{:S(2)}, u32[]{:S(2)}) collective-permute-start(f32[256,128]{1,0:T(8,128)S(1)} %get-tuple-element.57), channel_id=1, source_target_pairs={{0,6},{1,7},{2,4},{3,5},{4,2},{5,3},{6,0},{7,1},{8,14},{9,15},{10,... | collective-permute-start | bytes 393224 | tf_op jit(solution)/shard_map/ppermute | solution.py:40
  94.3 12.3 %collective-permute-start.28 = (f32[256,128]{1,0:T(8,128)S(1)}, f32[256,128]{1,0:T(8,128)S(1)}, u32[]{:S(2)}, u32[]{:S(2)}) collective-permute-start(f32[256,128]{1,0:T(8,128)S(1)} %get-tuple-element.63.refs_3_.refs_0_), channel_id=1, source_target_pairs={{0,8},{1,9},{2,10},{3,11},{4,12},{5,13},{6,14},{7,15},{8,0},{9,1},... | collective-permute-start | bytes 393224 | tf_op jit(solution)/shard_map/ppermute | solution.py:40
  97.6 9.1 %collective-permute-start.31 = (f32[256,128]{1,0:T(8,128)S(1)}, f32[256,128]{1,0:T(8,128)S(1)}, u32[]{:S(2)}, u32[]{:S(2)}) collective-permute-start(f32[256,128]{1,0:T(8,128)S(1)} %get-tuple-element.63.refs_3_.refs_0_), channel_id=1, source_target_pairs={{0,2},{1,3},{2,0},{3,1},{4,6},{5,7},{6,4},{7,5},{8,10},{9,11},{10,... | collective-permute-start | bytes 393224 | tf_op jit(solution)/shard_map/ppermute | solution.py:40
  97.6 9.1 %collective-permute-start.32 = (f32[256,128]{1,0:T(8,128)S(1)}, f32[256,128]{1,0:T(8,128)S(1)}, u32[]{:S(2)}, u32[]{:S(2)}) collective-permute-start(f32[256,128]{1,0:T(8,128)S(1)} %get-tuple-element.63.refs_3_.refs_0_), channel_id=1, source_target_pairs={{0,4},{1,5},{2,6},{3,7},{4,0},{5,1},{6,2},{7,3},{8,12},{9,13},{10,... | collective-permute-start | bytes 393224 | tf_op jit(solution)/shard_map/ppermute | solution.py:40
  100.4 6.7 %collective-permute-start.33 = (f32[256,128]{1,0:T(8,128)S(1)}, f32[256,128]{1,0:T(8,128)S(1)}, u32[]{:S(2)}, u32[]{:S(2)}) collective-permute-start(f32[256,128]{1,0:T(8,128)S(1)} %get-tuple-element.63.refs_3_.refs_0_), channel_id=1, source_target_pairs={{0,6},{1,7},{2,4},{3,5},{4,2},{5,3},{6,0},{7,1},{8,14},{9,15},{10,... | collective-permute-start | bytes 393224 | tf_op jit(solution)/shard_map/ppermute | solution.py:40
  107.2 4.9 %collective-permute-start.34 = (f32[4,256,128]{2,1,0:T(8,128)S(1)}, f32[4,256,128]{2,1,0:T(8,128)S(1)}, u32[]{:S(2)}, u32[]{:S(2)}) collective-permute-start(f32[4,256,128]{2,1,0:T(8,128)S(1)} %stack.21.near), channel_id=1, source_target_pairs={{0,1},{1,0},{2,3},{3,2},{4,5},{5,4},{6,7},{7,6},{8,9},{9,8},{10,11... | collective-permute-start | bytes 1572872 | tf_op jit(solution)/shard_map/ppermute | solution.py:40
  107.3 7.7 %collective-permute-start.36 = (f32[256,128]{1,0:T(8,128)S(1)}, f32[256,128]{1,0:T(8,128)S(1)}, u32[]{:S(2)}, u32[]{:S(2)}) collective-permute-start(f32[256,128]{1,0:T(8,128)S(1)} %collective-permute-done.28.refs_4_.refs_0_), channel_id=1, source_target_pairs={{0,2},{1,3},{2,0},{3,1},{4,6},{5,7},{6,4},{7,5},{8,10},{9,11},{10,... | collective-permute-start | bytes 393224 | tf_op jit(solution)/shard_map/ppermute | solution.py:40
  107.4 10.7 %collective-permute-start.29 = (f32[256,128]{1,0:T(8,128)S(1)}, f32[256,128]{1,0:T(8,128)S(1)}, u32[]{:S(2)}, u32[]{:S(2)}) collective-permute-start(f32[256,128]{1,0:T(8,128)S(1)} %collective-permute-done.28.refs_4_.refs_0_), channel_id=1, source_target_pairs={{0,4},{1,5},{2,6},{3,7},{4,0},{5,1},{6,2},{7,3},{8,12},{9,13},{10,... | collective-permute-start | bytes 393224 | tf_op jit(solution)/shard_map/ppermute | solution.py:40
  111.1 9.1 %collective-permute-start.30 = (f32[256,128]{1,0:T(8,128)S(1)}, f32[256,128]{1,0:T(8,128)S(1)}, u32[]{:S(2)}, u32[]{:S(2)}) collective-permute-start(f32[256,128]{1,0:T(8,128)S(1)} %collective-permute-done.28.refs_4_.refs_0_), channel_id=1, source_target_pairs={{0,6},{1,7},{2,4},{3,5},{4,2},{5,3},{6,0},{7,1},{8,14},{9,15},{10,... | collective-permute-start | bytes 393224 | tf_op jit(solution)/shard_map/ppermute | solution.py:40
  115.0 5.3 %collective-permute-start.37 = (f32[2,256,128]{2,1,0:T(8,128)S(1)}, f32[2,256,128]{2,1,0:T(8,128)S(1)}, u32[]{:S(2)}, u32[]{:S(2)}) collective-permute-start(f32[2,256,128]{2,1,0:T(8,128)S(1)} %stack.23.near), channel_id=1, source_target_pairs={{0,1},{1,0},{2,3},{3,2},{4,5},{5,4},{6,7},{7,6},{8,9},{9,8},{10,11... | collective-permute-start | bytes 786440 | tf_op jit(solution)/shard_map/ppermute | solution.py:40
  120.2 3.0 %collective-permute-start.35 = (f32[2,256,128]{2,1,0:T(8,128)S(1)}, f32[2,256,128]{2,1,0:T(8,128)S(1)}, u32[]{:S(2)}, u32[]{:S(2)}) collective-permute-start(f32[2,256,128]{2,1,0:T(8,128)S(1)} %stack.22.near), channel_id=1, source_target_pairs={{0,1},{1,0},{2,3},{3,2},{4,5},{5,4},{6,7},{7,6},{8,9},{9,8},{10,11... | collective-permute-start | bytes 786440 | tf_op jit(solution)/shard_map/ppermute | solution.py:40
  124.0 10.7 %collective-permute-start.38 = (f32[512,128]{1,0:T(8,128)S(1)}, f32[512,128]{1,0:T(8,128)S(1)}, u32[]{:S(2)}, u32[]{:S(2)}) collective-permute-start(f32[512,128]{1,0:T(8,128)S(1)} %predict.11), channel_id=1, source_target_pairs={{0,128},{16,144},{32,160},{48,176},{64,192},{80,208},{96,224},{112... | collective-permute-start | bytes 786440 | tf_op jit(solution)/shard_map/ppermute | solution.py:40
  125.0 15.0 %collective-permute-start.40 = (f32[512,128]{1,0:T(8,128)S(1)}, f32[512,128]{1,0:T(8,128)S(1)}, u32[]{:S(2)}, u32[]{:S(2)}) collective-permute-start(f32[512,128]{1,0:T(8,128)S(1)} %predict.13), channel_id=1, source_target_pairs={{0,192},{16,208},{32,224},{48,240},{64,128},{80,144},{96,160},{112... | collective-permute-start | bytes 786440 | tf_op jit(solution)/shard_map/ppermute | solution.py:40
  127.6 12.3 %collective-permute-start.39 = (f32[512,128]{1,0:T(8,128)S(1)}, f32[512,128]{1,0:T(8,128)S(1)}, u32[]{:S(2)}, u32[]{:S(2)}) collective-permute-start(f32[512,128]{1,0:T(8,128)S(1)} %predict.12), channel_id=1, source_target_pairs={{0,64},{16,80},{32,96},{48,112},{64,0},{80,16},{96,32},{112,48},{1... | collective-permute-start | bytes 786440 | tf_op jit(solution)/shard_map/ppermute | solution.py:40
  140.0 4.9 %collective-permute-start.41 = (f32[128,128]{1,0:T(8,128)S(1)}, f32[128,128]{1,0:T(8,128)S(1)}, u32[]{:S(2)}, u32[]{:S(2)}) collective-permute-start(f32[128,128]{1,0:T(8,128)S(1)} %get-tuple-element.79), channel_id=1, source_target_pairs={{0,16},{16,0},{32,48},{48,32},{64,80},{80,64},{96,112},{112,96},{1... | collective-permute-start | bytes 196616 | tf_op jit(solution)/shard_map/ppermute | solution.py:40
  140.7 6.5 %collective-permute-start.42 = (f32[128,128]{1,0:T(8,128)S(1)}, f32[128,128]{1,0:T(8,128)S(1)}, u32[]{:S(2)}, u32[]{:S(2)}) collective-permute-start(f32[128,128]{1,0:T(8,128)S(1)} %get-tuple-element.80), channel_id=1, source_target_pairs={{0,32},{16,48},{32,0},{48,16},{64,96},{80,112},{96,64},{112,80},{1... | collective-permute-start | bytes 196616 | tf_op jit(solution)/shard_map/ppermute | solution.py:40
  142.5 7.0 %collective-permute-start.43 = (f32[128,128]{1,0:T(8,128)S(1)}, f32[128,128]{1,0:T(8,128)S(1)}, u32[]{:S(2)}, u32[]{:S(2)}) collective-permute-start(f32[128,128]{1,0:T(8,128)S(1)} %get-tuple-element.81), channel_id=1, source_target_pairs={{0,48},{16,32},{32,16},{48,0},{64,112},{80,96},{96,80},{112,64},{1... | collective-permute-start | bytes 196616 | tf_op jit(solution)/shard_map/ppermute | solution.py:40
  (1 other events, 1.8 us)
